TPU v7x, 128 devices: a whole 4x4x4 slice. The times are simulated.
128 devices in a mesh: dp: 64 (over y, x_hi, z, core), tensor: 2 (over x_lo).
Axes of the slice: x: 4 (x_hi: 2, x_lo: 2; x = x_hi * 2 + x_lo), y: 4, z: 4, core: 2. Of those that a mesh axis runs over, the one named last changes fastest.
Arguments:
- layer_input: bfloat16 [32768, 768], P(('dp', 'tensor')), may hold values from -24 to 24
- segment_starts: int32 [32768], P('dp'), may hold values from 0 to 511, as said below
- norm_gains: bfloat16 [2, 768], P(None, 'dp'), may hold values from 0.5 to 1.5
- norm_shifts: bfloat16 [2, 768], P(None, 'dp'), may hold values from -3 to 3
- projection: bfloat16 [768, 3, 768], P('dp', None, 'tensor'), may hold values from -0.3125 to 0.3125
- triple_bias: bfloat16 [3, 768], P(None, ('tensor', 'dp')), may hold values from -3 to 3
- dense_weight: bfloat16 [768, 768], P('tensor', 'dp'), may hold values from -0.625 to 0.625
- inner_weight: bfloat16 [768, 3072], P('dp', 'tensor'), may hold values from -0.21875 to 0.21875
- unit_bias: bfloat16 [3072], P(('tensor', 'dp')), may hold values from -3 to 3
- outer_weight: bfloat16 [3072, 768], P('tensor', 'dp'), may hold values from -0.15625 to 0.15625
- final_bias: bfloat16 [768], P('dp'), may hold values from -3 to 3
- cotangent: bfloat16 [32768, 768], P(('dp', 'tensor')), may hold values from -24 to 24
Outputs:
- layer_output: bfloat16 [32768, 768], P(('dp', 'tensor'))
- input_grad: bfloat16 [32768, 768], P(('dp', 'tensor'))
- gains_grad: float32 [2, 768], P(None, ('dp', 'tensor'))
- shifts_grad: float32 [2, 768], P(None, ('dp', 'tensor'))
- projection_grad: float32 [768, 3, 768], P('dp', None, 'tensor')
- triple_grad: float32 [3, 768], P(None, ('tensor', 'dp'))
- dense_grad: float32 [768, 768], P('tensor', 'dp')
- inner_grad: float32 [768, 3072], P('dp', 'tensor')
- units_grad: float32 [3072], P(('tensor', 'dp'))
- outer_grad: float32 [3072, 768], P('tensor', 'dp')
- final_grad: float32 [768], P(('dp', 'tensor'))
Inputs may be any that keep to these rules, and one draw needn't show every extreme that they name: `segment_starts`: each token's entry is the index, within its group of 512 consecutive tokens, of the first token of its sequence; sequences never cross groups and hold at most 512 tokens, and some sequence holds exactly 512.
All inputs are finite; a program needn't handle non-finite values.
Results may differ from a plain program's by a relative error of at most 0.011.
Values may be sent and summed in bfloat16 or wider, within the bound.
A program may use at most 128 MiB of HBM per device.

v0:
```python
import math

import jax
import jax.numpy as jnp
from jax import lax
from jax.sharding import PartitionSpec as P

HD = 64
ROT = 16


EPSILON = 1e-05
BLOCK_ROWS = 512


def product(form, left, right):
    return jnp.einsum(form, left, right, preferred_element_type=jnp.float32)


def normalize(field):
    center = jnp.mean(field, axis=-1, keepdims=True)
    centred = field - center
    spread = jnp.mean(centred * centred, axis=-1, keepdims=True)
    factor = lax.rsqrt(spread + EPSILON)
    return (centred * factor, factor)


def angles_for(starts):
    group_size = starts.shape[0]
    places = (jnp.arange(group_size, dtype=jnp.int32) - starts).astype(jnp.float32)
    freqs = jnp.exp(jnp.arange(ROT // 2, dtype=jnp.float32) * (-2.0 * math.log(10000.0) / ROT))
    turns = places[:, None] * freqs[None, :]
    return (jnp.cos(turns)[:, None, :], jnp.sin(turns)[:, None, :])


def rotate(field, cosine_table, sine_table):
    half_rot = ROT // 2
    first = field[..., :half_rot]
    second = field[..., half_rot:ROT]
    return jnp.concatenate(
        [
            first * cosine_table - second * sine_table,
            second * cosine_table + first * sine_table,
            field[..., ROT:],
        ],
        axis=-1,
    )


def rotate_back(field, cosine_table, sine_table):
    half_rot = ROT // 2
    first = field[..., :half_rot]
    second = field[..., half_rot:ROT]
    return jnp.concatenate(
        [
            first * cosine_table + second * sine_table,
            second * cosine_table - first * sine_table,
            field[..., ROT:],
        ],
        axis=-1,
    )


def local(
    layer_input,
    segment_starts,
    norm_gains,
    norm_shifts,
    projection,
    triple_bias,
    dense_weight,
    inner_weight,
    unit_bias,
    outer_weight,
    final_bias,
    cotangent,
):
    (
        gains_full,
        shifts_full,
        triple_full,
        bias_triple,
        dense_full,
        inner_full,
        bias_inner,
        outer_full,
        bias_final,
    ) = (
        lax.all_gather(norm_gains, "dp", axis=1, tiled=True),
        lax.all_gather(norm_shifts, "dp", axis=1, tiled=True),
        lax.all_gather(projection, "dp", axis=0, tiled=True),
        lax.all_gather(triple_bias, "dp", axis=1, tiled=True),
        lax.all_gather(dense_weight, "dp", axis=1, tiled=True),
        lax.all_gather(inner_weight, "dp", axis=0, tiled=True),
        lax.all_gather(unit_bias, "dp", axis=0, tiled=True),
        lax.all_gather(outer_weight, "dp", axis=1, tiled=True),
        lax.all_gather(final_bias, "dp", axis=0, tiled=True),
    )
    residual = layer_input.astype(jnp.float32)
    normal_rows, factor = normalize(residual)
    gains_float = gains_full.astype(jnp.float32)
    shifts_float = shifts_full.astype(jnp.float32)
    first_in = (normal_rows * gains_float[0] + shifts_float[0]).astype(jnp.bfloat16)
    second_in = (normal_rows * gains_float[1] + shifts_float[1]).astype(jnp.bfloat16)
    first_all, second_all = (
        lax.all_gather(first_in, "tensor", axis=0, tiled=True),
        lax.all_gather(second_in, "tensor", axis=0, tiled=True),
    )
    group_size = first_all.shape[0]
    local_width = triple_full.shape[2]
    head_count = local_width // HD
    cosine_table, sine_table = angles_for(segment_starts)
    triple = (
        product("td,dke->kte", first_all, triple_full) + bias_triple.astype(jnp.float32)[:, None, :]
    )
    queries = rotate(
        triple[0].reshape(group_size, head_count, HD), cosine_table, sine_table
    ).astype(jnp.bfloat16)
    key_rows = rotate(
        triple[1].reshape(group_size, head_count, HD), cosine_table, sine_table
    ).astype(jnp.bfloat16)
    values = triple[2].reshape(group_size, head_count, HD).astype(jnp.bfloat16)
    block_rows = min(BLOCK_ROWS, group_size)
    block_count = group_size // block_rows
    score_scale = 1.0 / math.sqrt(HD)
    places = jnp.arange(group_size, dtype=jnp.int32)

    def scores_for():
        allowed = (segment_starts[:, None] == segment_starts[None, :]) & (
            places[None, :] <= places[:, None]
        )
        raw_scores = product("qhd,khd->hqk", queries, key_rows) * score_scale
        return (jnp.where(allowed[None], raw_scores, -1e30), queries)

    def attend(block_index):
        scores, unused_block = scores_for()
        row_peak = jnp.max(scores, axis=-1, keepdims=True)
        powers = jnp.exp(scores - row_peak)
        row_total = jnp.sum(powers, axis=-1, keepdims=True)
        probs_low = (powers / row_total).astype(jnp.bfloat16)
        result = product("hqk,khd->qhd", probs_low, values)
        return (result, (row_peak + jnp.log(row_total))[..., 0])

    context, logsum = lax.map(attend, jnp.arange(block_count, dtype=jnp.int32))
    context = context.reshape(group_size, local_width).astype(jnp.bfloat16)
    attend_part = product("te,ed->td", context, dense_full)
    inner_pre = product("td,df->tf", second_all, inner_full) + bias_inner.astype(jnp.float32)
    active = jax.nn.gelu(inner_pre, approximate=False).astype(jnp.bfloat16)
    feed_part = product("tf,fd->td", active, outer_full)
    attend_rows, feed_rows = (
        lax.psum_scatter(
            attend_part.astype(jnp.bfloat16), "tensor", scatter_dimension=0, tiled=True
        ).astype(jnp.float32),
        lax.psum_scatter(
            feed_part.astype(jnp.bfloat16), "tensor", scatter_dimension=0, tiled=True
        ).astype(jnp.float32),
    )
    layer_output = residual + attend_rows + feed_rows + bias_final.astype(jnp.float32)
    layer_output = layer_output.astype(jnp.bfloat16)
    gains_back, triple_back_weight, dense_back, inner_back, outer_back = (
        lax.all_gather(norm_gains, "dp", axis=1, tiled=True),
        lax.all_gather(projection, "dp", axis=0, tiled=True),
        lax.all_gather(dense_weight, "dp", axis=1, tiled=True),
        lax.all_gather(inner_weight, "dp", axis=0, tiled=True),
        lax.all_gather(outer_weight, "dp", axis=1, tiled=True),
    )
    upstream = cotangent.astype(jnp.float32)
    upstream_all = lax.all_gather(cotangent, "tensor", axis=0, tiled=True)
    final_term = jnp.sum(upstream, axis=0)
    outer_term = product("tf,td->fd", active, upstream_all)
    dense_term = product("te,td->ed", context, upstream_all)
    active_back = product("td,fd->tf", upstream_all, outer_back)
    gelu_slope = 0.5 * (1.0 + lax.erf(inner_pre * (1.0 / math.sqrt(2.0)))) + inner_pre * jnp.exp(
        -0.5 * inner_pre * inner_pre
    ) * (1.0 / math.sqrt(2.0 * math.pi))
    unit_back = (active_back * gelu_slope).astype(jnp.bfloat16)
    units_term = jnp.sum(unit_back.astype(jnp.float32), axis=0)
    inner_term = product("td,tf->df", second_all, unit_back)
    second_part = product("tf,df->td", unit_back, inner_back)
    context_back = product("td,ed->te", upstream_all, dense_back).astype(jnp.bfloat16)
    context_back = context_back.reshape(group_size, head_count, HD)

    def backward_block(carried, block_index):
        key_back, values_back = carried
        scores, query_block = scores_for()
        block_logsum = lax.dynamic_index_in_dim(logsum, block_index, 0, keepdims=False)
        probs = jnp.exp(scores - block_logsum[..., None])
        probs_low = probs.astype(jnp.bfloat16)
        values_back = values_back + product("hqk,qhd->khd", probs_low, context_back)
        prob_back = product("qhd,khd->hqk", context_back, values)
        inner_sum = jnp.sum(probs * prob_back, axis=-1, keepdims=True)
        score_back = (probs * (prob_back - inner_sum)).astype(jnp.bfloat16)
        query_back = product("hqk,khd->qhd", score_back, key_rows) * score_scale
        key_back = key_back + product("hqk,qhd->khd", score_back, query_block) * score_scale
        return ((key_back, values_back), query_back)

    zero_rows = jnp.zeros((group_size, head_count, HD), jnp.float32)
    (key_back, values_back), query_back = lax.scan(
        backward_block, (zero_rows, zero_rows), jnp.arange(block_count, dtype=jnp.int32)
    )
    query_back = query_back.reshape(group_size, head_count, HD)
    triple_back = jnp.stack(
        [
            rotate_back(query_back, cosine_table, sine_table).reshape(group_size, local_width),
            rotate_back(key_back, cosine_table, sine_table).reshape(group_size, local_width),
            values_back.reshape(group_size, local_width),
        ]
    ).astype(jnp.bfloat16)
    triple_term = jnp.sum(triple_back.astype(jnp.float32), axis=1)
    projection_term = product("td,kte->dke", first_all, triple_back)
    first_part = product("kte,dke->td", triple_back, triple_back_weight)
    first_back, second_back = (
        lax.psum_scatter(first_part, "tensor", scatter_dimension=0, tiled=True),
        lax.psum_scatter(second_part, "tensor", scatter_dimension=0, tiled=True),
    )
    gains_term = jnp.stack(
        [jnp.sum(first_back * normal_rows, axis=0), jnp.sum(second_back * normal_rows, axis=0)]
    )
    shifts_term = jnp.stack([jnp.sum(first_back, axis=0), jnp.sum(second_back, axis=0)])
    gains_back_float = gains_back.astype(jnp.float32)
    normal_back = first_back * gains_back_float[0] + second_back * gains_back_float[1]
    input_grad = upstream + factor * (
        normal_back
        - jnp.mean(normal_back, axis=-1, keepdims=True)
        - normal_rows * jnp.mean(normal_back * normal_rows, axis=-1, keepdims=True)
    )
    projection_grad, triple_grad, dense_grad, inner_grad, units_grad, outer_grad = (
        lax.psum_scatter(projection_term, "dp", scatter_dimension=0, tiled=True),
        lax.psum_scatter(triple_term, "dp", scatter_dimension=1, tiled=True),
        lax.psum_scatter(dense_term, "dp", scatter_dimension=1, tiled=True),
        lax.psum_scatter(inner_term, "dp", scatter_dimension=0, tiled=True),
        lax.psum_scatter(units_term, "dp", scatter_dimension=0, tiled=True),
        lax.psum_scatter(outer_term, "dp", scatter_dimension=1, tiled=True),
    )
    gains_grad, shifts_grad, final_grad = (
        lax.psum_scatter(gains_term, ("dp", "tensor"), scatter_dimension=1, tiled=True),
        lax.psum_scatter(shifts_term, ("dp", "tensor"), scatter_dimension=1, tiled=True),
        lax.psum_scatter(final_term, ("dp", "tensor"), scatter_dimension=0, tiled=True),
    )
    return (
        layer_output,
        input_grad.astype(jnp.bfloat16),
        gains_grad,
        shifts_grad,
        projection_grad,
        triple_grad,
        dense_grad,
        inner_grad,
        units_grad,
        outer_grad,
        final_grad,
    )


def solution(mesh):
    placed = (
        P(("dp", "tensor"), None),
        P("dp"),
        P(None, "dp"),
        P(None, "dp"),
        P("dp", None, "tensor"),
        P(None, ("tensor", "dp")),
        P("tensor", "dp"),
        P("dp", "tensor"),
        P(("tensor", "dp")),
        P("tensor", "dp"),
        P("dp"),
        P(("dp", "tensor"), None),
    )
    return jax.shard_map(
        local,
        mesh=mesh,
        in_specs=placed,
        out_specs=(
            P(("dp", "tensor"), None),
            P(("dp", "tensor"), None),
            P(None, ("dp", "tensor")),
            P(None, ("dp", "tensor")),
            P("dp", None, "tensor"),
            P(None, ("tensor", "dp")),
            P("tensor", "dp"),
            P("dp", "tensor"),
            P(("tensor", "dp")),
            P("tensor", "dp"),
            P(("dp", "tensor")),
        ),
        check_vma=False,
    )
```

profile of v0, /device:TPU:1, one launch (start us, length us, event | category | flops | bytes accessed | tf_op | source)
XLA Modules:
  0.0 1457.5 jit_solution(15385728972777059146)
XLA Ops:
  11.8 11.3 all_gather.52
  23.2 101.3 %all-gather.3 = bf16[64,12,384]{2,1,0:T(8,128)(2,1)S(1)} all-gather(bf16[1,12,384]{2,1,0:T(8,128)(2,1)} %bitcast.112), channel_id=1, replica_groups=mesh['dp'=64,'tensor'=2] {'dp'}, dimensions={0}, use_global_device_ids=true | all-gather | bytes 599040 | tf_op jit(solution)/shard_map/all_gather | solution.py:93
  124.6 88.6 %all-gather.2 = bf16[64,6,3]{1,2,0:T(4,128)(2,1)S(1)} all-gather(bf16[1,6,3]{1,2,0:T(4,128)(2,1)S(1)} %bitcast.114), channel_id=1, replica_groups=mesh['dp'=64,'tensor'=2] {'dp'}, dimensions={0}, use_global_device_ids=true | all-gather | bytes 2340 | tf_op jit(solution)/shard_map/all_gather | solution.py:92
  213.6 89.4 %all-gather.1 = bf16[64,12,2]{1,2,0:T(2,128)(2,1)S(1)} all-gather(bf16[1,12,2]{1,2,0:T(2,128)(2,1)S(1)} %bitcast.115), channel_id=1, replica_groups=mesh['dp'=64,'tensor'=2] {'dp'}, dimensions={0}, use_global_device_ids=true | all-gather | bytes 3120 | tf_op jit(solution)/shard_map/all_gather | solution.py:90
  303.4 88.1 %all-gather = bf16[64,12,2]{1,2,0:T(2,128)(2,1)S(1)} all-gather(bf16[1,12,2]{1,2,0:T(2,128)(2,1)S(1)} %bitcast.116), channel_id=1, replica_groups=mesh['dp'=64,'tensor'=2] {'dp'}, dimensions={0}, use_global_device_ids=true | all-gather | bytes 3120 | tf_op jit(solution)/shard_map/all_gather | solution.py:89
  393.4 11.5 all_gather.43
  435.4 165.1 %all-reduce.16 = (bf16[1536]{0:T(1024)(128)(2,1)S(1)}, bf16[768]{0:T(1024)(128)(2,1)S(1)}) all-reduce(bf16[1536]{0:T(1024)(128)(2,1)S(1)} %dynamic-update-slice, bf16[768]{0:T(1024)(128)(2,1)S(1)} %dynamic-update-slice.1), channel_id=1, replica_groups=mesh['dp'=64,'tensor'=2] {'dp'}, use_global_device_ids=true, to_apply=%add | all-reduce | flops 2304 | bytes 9216
  600.5 10.9 all_gather.47
  615.9 4.9 reshape.176
  620.8 4.9 reshape.178
  625.6 10.2 fusion.7
  649.1 5.1 fusion.70
  657.9 190.5 %fusion.64 = (f32[384,16]{0,1:T(8,128)}, f32[16,1536]{1,0:T(8,128)}, f32[1536,16]{0,1:T(8,128)}) fusion(f32[384,768]{0,1:T(8,128)S(1)} %fusion.69, f32[768,1536]{1,0:T(8,128)} %fusion.70, f32[1536,768]{0,1:T(8,128)} %fusion.71), kind=kCustom, calls=%all-reduce-scatter.3 | all-reduce-scatter fusion | flops 3538945 | bytes 10838528
  857.0 13.8 collective-permute-start.9
  874.7 4.9 collective-permute-start.6
  903.1 4.9 collective-permute-start.29
  927.3 5.3 collective-permute-start.20
  932.7 8.2 collective-permute-start.19
  956.9 7.3 collective-permute-start.45
  974.5 316.4 %all-reduce.15 = (f32[3,384]{1,0:T(4,128)S(1)}, f32[1536]{0:T(1024)S(1)}) all-reduce(f32[3,384]{1,0:T(4,128)S(1)} %convert_reduce_fusion.1, f32[1536]{0:T(1024)S(1)} %get-tuple-element.171), channel_id=9, replica_groups=mesh['dp'=64,'tensor'=2] {'dp'}, use_global_device_ids=true, to_apply=%region_19.20.clone | all-reduce | flops 2688 | bytes 21504
  1298.7 11.0 concatenate.20
  1322.1 6.6 concatenate.21
  1328.8 26.4 %concatenate.22 = f32[1536,268]{0,1:T(8,128)} concatenate(f32[1536,12]{0,1:T(8,128)S(1)} %collective-permute-done.47, f32[1536,16]{0,1:T(8,128)S(1)} %collective-permute-done.46, f32[1536,16]{0,1:T(8,128)} %collective-permute-done.45, f32[1536,16]{0,1:T(8,128)} %collective-permute-done.44, f32[1536,16]{0,1:T(8,128)} %collective-permute-done.43, ...), dimensions={1} | concatenate | bytes 3293184
  1363.6 84.8 %all-reduce.14 = (f32[2,768]{1,0:T(2,128)S(1)}, f32[2,768]{1,0:T(2,128)S(1)}, f32[768]{0:T(1024)S(1)}) all-reduce(f32[2,768]{1,0:T(2,128)S(1)} %pad_maximum_fusion.9, f32[2,768]{1,0:T(2,128)S(1)} %pad_maximum_fusion.10, f32[768]{0:T(1024)S(1)} %get-tuple-element.153), channel_id=6, replica_groups=mesh['dp'=64,'tensor'=2] {'dp','tensor'}, use_global_device_ids=true, to_apply=%region_13.14.clone | all-reduce | flops 3840 | bytes 30720
  (340 shorter events, 165.7 us)
Async XLA Ops:
  7.2 398.9 %all-gather.10.cloned.1.call-start = ((), (), s32[]{:S(2)}) async-start(), calls=%async_computation.4 | async-start | bytes 2396160 | tf_op jit(solution)/shard_map/all_gather | solution.py:91
  8.0 607.9 %all-gather.12.cloned.1.call-start = ((), (), s32[]{:S(2)}) async-start(), calls=%async_computation.9 | async-start | bytes 3194880 | tf_op jit(solution)/shard_map/all_gather | solution.py:94
  8.7 612.1 %all-gather.14.cloned.1.call-start = ((), (), s32[]{:S(2)}) async-start(), calls=%async_computation.10 | async-start | bytes 3194880 | tf_op jit(solution)/shard_map/all_gather | solution.py:96
  9.4 1348.0 %all-reduce.20.cloned.1.call-start = ((), (), s32[]{:S(2)}) async-start(), calls=%async_computation.11 | async-start | bytes 7077888
  432.4 926.7 %reduce-scatter.19.cloned.1.call-start = ((), (), s32[]{:S(2)}) async-start(), calls=%async_computation.7 | async-start | bytes 2359296 | tf_op jit(solution)/shard_map/reduce_scatter | solution.py:213
  615.8 743.3 %reduce-scatter.21.cloned.1.call-start = ((), (), s32[]{:S(2)}) async-start(), calls=%async_computation.8 | async-start | bytes 2359296 | tf_op jit(solution)/shard_map/reduce_scatter | solution.py:214
  641.9 719.3 %reduce-scatter.15.cloned.1.call-start = ((), (), s32[]{:S(2)}) async-start(), calls=%async_computation.5 | async-start | bytes 1179648 | tf_op jit(solution)/shard_map/reduce_scatter | solution.py:151
  649.1 712.1 %reduce-scatter.17.cloned.1.call-start = ((), (), s32[]{:S(2)}) async-start(), calls=%async_computation.6 | async-start | bytes 1179648 | tf_op jit(solution)/shard_map/reduce_scatter | solution.py:154
  855.7 24.9 %collective-permute-start.10 = (f32[384,16]{0,1:T(8,128)}, f32[384,16]{0,1:T(8,128)S(1)}, u32[]{:S(2)}, u32[]{:S(2)}) collective-permute-start(f32[384,16]{0,1:T(8,128)} %get-tuple-element.132), channel_id=1, source_target_pairs={{0,22},{2,24},{4,26},{6,28},{8,30},{10,32},{12,34},{14,36},{16,38}... | collective-permute-start | bytes 73736
  857.0 24.9 %collective-permute-start.9 = (f32[384,16]{0,1:T(8,128)}, f32[384,16]{0,1:T(8,128)S(1)}, u32[]{:S(2)}, u32[]{:S(2)}) collective-permute-start(f32[384,16]{0,1:T(8,128)} %get-tuple-element.132), channel_id=1, source_target_pairs={{0,20},{2,22},{4,24},{6,26},{8,28},{10,30},{12,32},{14,34},{16,36}... | collective-permute-start | bytes 73736
  880.5 28.7 %collective-permute-start.31 = (f32[12,1536]{1,0:T(8,128)S(1)}, f32[12,1536]{1,0:T(8,128)S(1)}, u32[]{:S(2)}, u32[]{:S(2)}) collective-permute-start(f32[12,1536]{1,0:T(8,128)S(1)} %slice.103), channel_id=1, source_target_pairs={{0,32},{2,34},{4,36},{6,38},{8,40},{10,42},{12,44},{14,46},{16,48}... | collective-permute-start | bytes 221192
  881.9 28.7 %collective-permute-start.47 = (f32[1536,12]{0,1:T(8,128)S(1)}, f32[1536,12]{0,1:T(8,128)S(1)}, u32[]{:S(2)}, u32[]{:S(2)}) collective-permute-start(f32[1536,12]{0,1:T(8,128)S(1)} %slice.104), channel_id=1, source_target_pairs={{0,32},{2,34},{4,36},{6,38},{8,40},{10,42},{12,44},{14,46},{16,48}... | collective-permute-start | bytes 221192
  919.0 21.9 %collective-permute-start.23 = (f32[16,1536]{1,0:T(8,128)}, f32[16,1536]{1,0:T(8,128)S(1)}, u32[]{:S(2)}, u32[]{:S(2)}) collective-permute-start(f32[16,1536]{1,0:T(8,128)} %get-tuple-element.133), channel_id=1, source_target_pairs={{0,16},{2,18},{4,20},{6,22},{8,24},{10,26},{12,28},{14,30},{16,32}... | collective-permute-start | bytes 294920
  922.1 23.1 %collective-permute-start.22 = (f32[16,1536]{1,0:T(8,128)}, f32[16,1536]{1,0:T(8,128)S(1)}, u32[]{:S(2)}, u32[]{:S(2)}) collective-permute-start(f32[16,1536]{1,0:T(8,128)} %get-tuple-element.133), channel_id=1, source_target_pairs={{0,14},{2,16},{4,18},{6,20},{8,22},{10,24},{12,26},{14,28},{16,30}... | collective-permute-start | bytes 294920
  926.0 21.1 %collective-permute-start.21 = (f32[16,1536]{1,0:T(8,128)}, f32[16,1536]{1,0:T(8,128)S(1)}, u32[]{:S(2)}, u32[]{:S(2)}) collective-permute-start(f32[16,1536]{1,0:T(8,128)} %get-tuple-element.133), channel_id=1, source_target_pairs={{0,12},{2,14},{4,16},{6,18},{8,20},{10,22},{12,24},{14,26},{16,28}... | collective-permute-start | bytes 294920
  927.3 26.3 %collective-permute-start.20 = (f32[16,1536]{1,0:T(8,128)}, f32[16,1536]{1,0:T(8,128)}, u32[]{:S(2)}, u32[]{:S(2)}) collective-permute-start(f32[16,1536]{1,0:T(8,128)} %get-tuple-element.133), channel_id=1, source_target_pairs={{0,10},{2,12},{4,14},{6,16},{8,18},{10,20},{12,22},{14,24},{16,26}... | collective-permute-start | bytes 294920
  932.7 24.3 %collective-permute-start.19 = (f32[16,1536]{1,0:T(8,128)}, f32[16,1536]{1,0:T(8,128)}, u32[]{:S(2)}, u32[]{:S(2)}) collective-permute-start(f32[16,1536]{1,0:T(8,128)} %get-tuple-element.133), channel_id=1, source_target_pairs={{0,8},{2,10},{4,12},{6,14},{8,16},{10,18},{12,20},{14,22},{16,24},... | collective-permute-start | bytes 294920
  940.9 23.4 %collective-permute-start.18 = (f32[16,1536]{1,0:T(8,128)}, f32[16,1536]{1,0:T(8,128)}, u32[]{:S(2)}, u32[]{:S(2)}) collective-permute-start(f32[16,1536]{1,0:T(8,128)} %get-tuple-element.133), channel_id=1, source_target_pairs={{0,6},{2,8},{4,10},{6,12},{8,14},{10,16},{12,18},{14,20},{16,22},{... | collective-permute-start | bytes 294920
  953.7 337.8 %collective-permute-start.46 = (f32[1536,16]{0,1:T(8,128)}, f32[1536,16]{0,1:T(8,128)S(1)}, u32[]{:S(2)}, u32[]{:S(2)}) collective-permute-start(f32[1536,16]{0,1:T(8,128)} %get-tuple-element.134), channel_id=1, source_target_pairs={{0,30},{2,32},{4,34},{6,36},{8,38},{10,40},{12,42},{14,44},{16,46}... | collective-permute-start | bytes 294920
  956.9 335.9 %collective-permute-start.45 = (f32[1536,16]{0,1:T(8,128)}, f32[1536,16]{0,1:T(8,128)}, u32[]{:S(2)}, u32[]{:S(2)}) collective-permute-start(f32[1536,16]{0,1:T(8,128)} %get-tuple-element.134), channel_id=1, source_target_pairs={{0,28},{2,30},{4,32},{6,34},{8,36},{10,38},{12,40},{14,42},{16,44}... | collective-permute-start | bytes 294920
  964.3 329.8 %collective-permute-start.44 = (f32[1536,16]{0,1:T(8,128)}, f32[1536,16]{0,1:T(8,128)}, u32[]{:S(2)}, u32[]{:S(2)}) collective-permute-start(f32[1536,16]{0,1:T(8,128)} %get-tuple-element.134), channel_id=1, source_target_pairs={{0,26},{2,28},{4,30},{6,32},{8,34},{10,36},{12,38},{14,40},{16,42}... | collective-permute-start | bytes 294920
  966.2 329.2 %collective-permute-start.43 = (f32[1536,16]{0,1:T(8,128)}, f32[1536,16]{0,1:T(8,128)}, u32[]{:S(2)}, u32[]{:S(2)}) collective-permute-start(f32[1536,16]{0,1:T(8,128)} %get-tuple-element.134), channel_id=1, source_target_pairs={{0,24},{2,26},{4,28},{6,30},{8,32},{10,34},{12,36},{14,38},{16,40}... | collective-permute-start | bytes 294920
  968.1 328.6 %collective-permute-start.42 = (f32[1536,16]{0,1:T(8,128)}, f32[1536,16]{0,1:T(8,128)}, u32[]{:S(2)}, u32[]{:S(2)}) collective-permute-start(f32[1536,16]{0,1:T(8,128)} %get-tuple-element.134), channel_id=1, source_target_pairs={{0,22},{2,24},{4,26},{6,28},{8,30},{10,32},{12,34},{14,36},{16,38}... | collective-permute-start | bytes 294920
  1296.7 22.2 %collective-permute-start.37 = (f32[1536,16]{0,1:T(8,128)S(1)}, f32[1536,16]{0,1:T(8,128)S(1)}, u32[]{:S(2)}, u32[]{:S(2)}) collective-permute-start(f32[1536,16]{0,1:T(8,128)S(1)} %copy-done.16), channel_id=1, source_target_pairs={{0,12},{2,14},{4,16},{6,18},{8,20},{10,22},{12,24},{14,26},{16,28}... | collective-permute-start | bytes 294920
  (103 other events, 5964.9 us)
Sparse Core Ops, SparseCore 0:
  11.2 72.2 all-gather.9
  86.8 66.7 all-gather.11
  156.9 67.6 all-gather.13
  432.5 640.6 all-reduce.19
  1075.5 27.8 reduce-scatter.18
  1105.6 29.5 reduce-scatter.20
  1137.7 20.7 reduce-scatter.14
  1160.9 20.8 reduce-scatter.16
where the time goes:
time: 1470 us; the launch traced here: 1460 us
  blocking collectives  1160 us (79%)
  starting transfers between devices  132 us (9%)
  local copies, waits for them, and re-layouts  73.7 us (5%)
  matrix products  56.4 us (4%)
  between operations  20.2 us (1%)
    unnamed x4, blocking collectives  757 us
    unnamed x49, starting transfers between devices  132 us
    all_gather x1, blocking collectives, local(): lax.all_gather(dense_weight, 'dp', axis=1, tiled=True)  101 us
    all_gather x1, blocking collectives, local(): lax.all_gather(norm_shifts, 'dp', axis=1, tiled=True)  89.4 us
    all_gather x1, blocking collectives, local(): lax.all_gather(triple_bias, 'dp', axis=1, tiled=True)  88.6 us
    all_gather x1, blocking collectives, local(): lax.all_gather(norm_gains, 'dp', axis=1, tiled=True)  88.1 us
    unnamed x166, local copies, waits for them, and re-layouts  69.9 us
    dot_general x18, matrix products, product(): return jnp.einsum(form, left, right, preferred_element_type=jnp.float32)  56.4 us
  transfers between devices with their start and end apart: 56, of which 0 were waited for; matrix products, arithmetic and copies ran while one was open for 22% of the time, Pallas kernels for 0%

commit v1 on v0

v1 whole, which is shorter than its diff:
```python
import math

import jax
import jax.numpy as jnp
import numpy as np
from jax import lax
from jax.experimental import pallas as pl
from jax.experimental.pallas import tpu as pltpu
from jax.sharding import PartitionSpec as P

MESH = pl.DeviceIdType.MESH
F32, BF16 = jnp.float32, jnp.bfloat16

D, HD, ROT = 768, 64, 16
T, HALF_T = 512, 256
EPSILON = 1e-05
Y, XH, Z, CORE = 4, 2, 4, 2
OWN = 12
PAD = 16
BLK = OWN * XH * CORE
PROJ, SMALL, DENSE, INNER, OUTER, COLS = 0, 1152, 1280, 1664, 3200, 4864
HALF = COLS // 2
PART = ((0, 1280), (1280, 1152))
CUT = ((0, 640, 640), (0, 640, 512))
VEC = 5 * D + 3 * 384 + 1536
OFF_TB, OFF_UB = 5 * OWN, 5 * OWN + 18
VMEM_LIMIT = 56 * 1024 * 1024


def order_tables():
    j = np.arange(64)
    c, xh, z, y = j % 2, (j // 2) % 2, (j // 4) % 4, j // 16
    dp = ((y * 2 + xh) * 4 + z) * 2 + c
    at = (12 * dp[:, None] + np.arange(12)[None, :]).reshape(-1)
    perm = np.zeros((D, D), np.float32)
    perm[at, np.arange(D)] = 1
    spread = np.zeros((128, VEC), np.float32)
    mask = np.zeros((64, VEC), np.float32)
    col = np.arange(D)
    for v in range(5):
        spread[v * 12 + col % 12, v * D + col] = 1
        mask[col // 12, v * D + col] = 1
    back = np.argsort(dp)
    col = np.arange(384)
    for k in range(3):
        spread[OFF_TB + 6 * k + col % 6, 5 * D + 384 * k + col] = 1
        mask[back[col // 6], 5 * D + 384 * k + col] = 1
    col = np.arange(1536)
    spread[OFF_UB + col % 24, 5 * D + 1152 + col] = 1
    mask[back[col // 24], 5 * D + 1152 + col] = 1
    rows = np.zeros((D, 64), np.float32)
    rows[12 * j, j] = 1
    pick = np.zeros((BLK, 64), np.float32)
    r = np.arange(BLK)
    pick[r, 16 * (r // 12) + r % 12] = 1
    return [m.astype(jnp.bfloat16) for m in (perm, spread, mask, rows, np.ascontiguousarray(rows.T), pick, np.ascontiguousarray(pick.T))]


def nn(a, b):
    return lax.dot_general(a, b, (((1,), (0,)), ((), ())), preferred_element_type=F32)


def nt(a, b):
    return lax.dot_general(a, b, (((1,), (1,)), ((), ())), preferred_element_type=F32)


def tn(a, b):
    return lax.dot_general(a, b, (((0,), (0,)), ((), ())), preferred_element_type=F32)


class Place:
    def __init__(self):
        dp = lax.axis_index("dp")
        self.t = lax.axis_index("tensor")
        self.c = lax.rem(dp, 2)
        self.z = lax.rem(lax.div(dp, 2), 4)
        self.xh = lax.rem(lax.div(dp, 8), 2)
        self.y = lax.div(dp, 16)
        self.slot = self.xh * 2 + self.c

    def dev(self, y=None, xh=None, z=None, c=None, t=None):
        y = self.y if y is None else y
        xh = self.xh if xh is None else xh
        z = self.z if z is None else z
        c = self.c if c is None else c
        t = self.t if t is None else t
        return (((y * 2 + xh) * 4 + z) * 2 + c, t)

    def ring(self, axis, step):
        at = lax.rem((self.y if axis == "y" else self.z) + step, 4)
        return self.dev(y=at) if axis == "y" else self.dev(z=at)

    def quad(self, r):
        c = 1 - self.c if r & 1 else self.c
        xh = 1 - self.xh if r & 2 else self.xh
        return self.dev(xh=xh, c=c), xh, c

    def peers(self):
        out = [self.quad(r)[0] for r in (1, 2, 3)]
        for axis in ("y", "z"):
            out += [self.ring(axis, 1), self.ring(axis, 3)]
        return out + [self.dev(t=1 - self.t)]


def enter(place):
    barrier = pltpu.get_barrier_semaphore()
    peers = place.peers()
    for peer in peers:
        pl.semaphore_signal(barrier, inc=1, device_id=peer, device_id_type=MESH)
    pl.semaphore_wait(barrier, len(peers))


def remote(src, dst, send, recv, device):
    copy = pltpu.make_async_remote_copy(
        src_ref=src, dst_ref=dst, send_sem=send, recv_sem=recv, device_id=device, device_id_type=MESH
    )
    copy.start()
    return copy


AXES = (("y", "z"), ("z", "y"))


def cols_of(core, part, piece=None):
    begin, width = PART[part]
    if piece is not None:
        first, second = CUT[part][1:]
        begin, width = (begin, first) if piece == 0 else (begin + first, second)
    return pl.ds(pl.multiple_of(core * HALF + begin, 128), width)


def gather_kernel(
    mine, x, cot, pick, w, xall, cotall, quad, blk, qsend, qrecv, rsend, rrecv, ssend, srecv, tsend, trecv, lsem
):
    me = Place()
    enter(me)
    partner = me.dev(t=1 - me.t)
    rows = pl.ds(pl.multiple_of(me.t * HALF_T, HALF_T), HALF_T)
    waits = []
    quads = []
    for r in (1, 2, 3):
        device, _, c = me.quad(r)
        quads.append(
            remote(
                mine.at[:, pl.ds(pl.multiple_of(c * HALF, 128), HALF)],
                quad.at[me.slot],
                qsend.at[r],
                qrecv.at[r],
                device,
            )
        )
    for i, (src, dst) in enumerate(((x, xall), (cot, cotall))):
        waits.append(remote(src, dst.at[rows], tsend.at[i], trecv.at[i], partner))
        local = pltpu.make_async_copy(src, dst.at[rows], lsem.at[i])
        local.start()
        waits.append(local)
    quad[me.slot] = mine[:, pl.ds(pl.multiple_of(me.c * HALF, 128), HALF)]
    for copy in quads:
        copy.wait_recv()
    blk[...] = nn(pick[...], quad[...].reshape(64, HALF)).astype(BF16)

    sibling = me.dev(c=1 - me.c)
    half = pl.ds(pl.multiple_of(me.c * HALF, 128), HALF)
    keep = pltpu.make_async_copy(blk, w.at[me.y, me.z, :, half], lsem.at[2])
    keep.start()
    waits.append(remote(blk, w.at[me.y, me.z, :, half], ssend.at[0], srecv.at[0], sibling))

    def share(index, ref):
        waits.append(remote(ref, ref, ssend.at[index], srecv.at[index], sibling))

    def unit(part, phase, step, piece=None):
        cols = cols_of(me.c, part, piece)
        axis = AXES[part][phase]
        y, z = me.y, me.z
        if axis == "y":
            y = lax.rem(y + step, 4)
        else:
            z = lax.rem(z + step, 4)
        if phase == 0:
            return w.at[y, z, :, cols]
        return w.at[y, :, :, cols] if axis == "y" else w.at[:, z, :, cols]

    for phase in range(2):
        copies = {}
        for part in range(2):
            axis = AXES[part][phase]
            for i, step in enumerate((1, 3)):
                src = unit(part, phase, 0)
                if phase == 0:
                    src = blk.at[:, pl.ds(*PART[part])]
                copies[part, i] = remote(
                    src,
                    unit(part, phase, 0),
                    rsend.at[part, phase, i],
                    rrecv.at[part, phase, i],
                    me.ring(axis, step),
                )
        for part in range(2):
            axis = AXES[part][phase]
            for i, step in enumerate((1, 3)):
                copies[part, i].wait_recv()
                ref = unit(part, phase, 4 - step, i)
                copies[part, 2 + i] = remote(
                    ref, ref, rsend.at[part, phase, 2 + i], rrecv.at[part, phase, 2 + i], me.ring(axis, step)
                )
        for part in range(2):
            for i, step in enumerate((1, 3)):
                share(1 + part * 6 + phase * 3 + i, unit(part, phase, 4 - step))
        for part in range(2):
            for i in range(2):
                copies[part, 2 + i].wait_recv()
            share(1 + part * 6 + phase * 3 + 2, unit(part, phase, 2))
        if phase == 0:
            keep.wait()
        for copy in copies.values():
            copy.wait_send()
    for copy in quads:
        copy.wait_send()
    for copy in waits:
        copy.wait()


def compute_kernel(
    w, x, cot, perm, spread, mask, rows_at, rows_of, cos_t, left_t, right_t, start_col, start_row,
    g, base_out, out_send, nb_own, nb_send, hat_own, fac_own, up_own,
    s1, s2, up, s1t, s2t, upt, hat, fac, q, k, v, cb, ctx, tb, act, ub, outp, nbp, vec, gvec,
):
    gvec[...] = jnp.zeros_like(gvec)
    small = nn(rows_of[...], w[:, SMALL:DENSE]).astype(BF16)
    for begin in range(0, VEC, D):
        width = min(D, VEC - begin)
        cols = slice(begin, begin + width)
        picked = nn(small, spread[:, cols]) * mask[:, cols].astype(F32)
        vec[:, cols] = jnp.broadcast_to(jnp.sum(picked, axis=0, keepdims=True), (8, width))

    def rowvec(begin, width):
        return vec[0:1, pl.ds(begin, width)]

    g0, g1, h0, h1, fb = (vec[0:1, i * D : (i + 1) * D] for i in range(5))

    def norm_rows(i, carry):
        rows = pl.ds(pl.multiple_of(i * 128, 128), 128)
        field = nn(x[rows, :], perm[...])
        center = jnp.mean(field, axis=-1, keepdims=True)
        centred = field - center
        factor = lax.rsqrt(jnp.mean(centred * centred, axis=-1, keepdims=True) + EPSILON)
        normal = centred * factor
        hat[rows, :] = normal
        fac[rows, :] = jnp.broadcast_to(factor, (128, 128))
        first = normal * g0 + h0
        second = normal * g1 + h1
        upstream = nn(cot[rows, :], perm[...])
        s1[rows, :] = first.astype(BF16)
        s2[rows, :] = second.astype(BF16)
        up[rows, :] = upstream.astype(BF16)
        outp[rows, :] = field + fb
        s1t[:, rows] = first.astype(BF16).T
        s2t[:, rows] = second.astype(BF16).T
        upt[:, rows] = upstream.astype(BF16).T
        gvec[0:1, 4 * D : 5 * D] += jnp.sum(upstream, axis=0, keepdims=True)
        return carry

    lax.fori_loop(0, 4, norm_rows, 0)

    def rotated(field, cosine, left, right, sign):
        n = field.shape[1]
        reps = n // 128
        wide = lambda table: jnp.concatenate([table] * reps, axis=1) if reps > 1 else table
        turned = pltpu.roll(field, n - 8, 1) * wide(left) + pltpu.roll(field, 8, 1) * wide(right)
        return field * wide(cosine) + sign * turned

    def heads_in(i, carry):
        cols = pl.ds(pl.multiple_of(i * 128, 128), 128)
        for n, ref in enumerate((q, k, v)):
            at = pl.ds(pl.multiple_of(PROJ + n * 384 + i * 128, 128), 128)
            field = nn(s1[...], w[:, at]) + rowvec(pl.multiple_of(5 * D + n * 384 + i * 128, 128), 128)
            if n < 2:
                field = rotated(field, cos_t[...], left_t[...], right_t[...], 1.0)
            ref[:, cols] = field.astype(BF16)
        cb[:, cols] = nn(up[...], w[:, pl.ds(pl.multiple_of(DENSE + i * 128, 128), 128)]).astype(BF16)
        return carry

    lax.fori_loop(0, 3, heads_in, 0)

    scale = 1.0 / math.sqrt(HD)

    def attend(pair, carry):
        cols = pl.ds(pl.multiple_of(pair * 128, 128), 128)
        halves = []
        for head in range(2):
            inside = (lax.broadcasted_iota(jnp.int32, (1, 128), 1) // HD) == head
            grads_k, grads_v, outs, grads_q = [], [], [], []
            for block in range(2):
                begin, n = block * HALF_T, (block + 1) * HALF_T
                rows = slice(begin, begin + HALF_T)
                kk, vv = k[0:n, cols], v[0:n, cols]
                qq = jnp.where(inside, q[rows, cols], 0).astype(BF16)
                cc = jnp.where(inside, cb[rows, cols], 0).astype(BF16)
                place_t = begin + lax.broadcasted_iota(jnp.int32, (HALF_T, n), 0)
                place_s = lax.broadcasted_iota(jnp.int32, (HALF_T, n), 1)
                allowed = (start_col[rows, 0:1] == start_row[0:1, 0:n]) & (place_s <= place_t)
                scores = jnp.where(allowed, nt(qq, kk) * scale, -1e30)
                powers = jnp.exp(scores - jnp.max(scores, axis=-1, keepdims=True))
                probs = powers / jnp.sum(powers, axis=-1, keepdims=True)
                low = probs.astype(BF16)
                outs.append(nn(low, vv))
                back = nt(cc, vv)
                inner = jnp.sum(probs * back, axis=-1, keepdims=True)
                ds = (probs * (back - inner)).astype(BF16)
                grads_q.append(nn(ds, kk) * scale)
                grads_k.append(tn(ds, qq) * scale)
                grads_v.append(tn(low, cc))
            join = lambda parts: jnp.concatenate([parts[1][:HALF_T] + parts[0], parts[1][HALF_T:]], axis=0)
            halves.append(
                (jnp.concatenate(outs, axis=0), jnp.concatenate(grads_q, axis=0), join(grads_k), join(grads_v))
            )
        first = (lax.broadcasted_iota(jnp.int32, (1, 128), 1) // HD) == 0
        out, dq, dk, dv = (jnp.where(first, a, b) for a, b in zip(*halves))
        ctx[:, cols] = out.astype(BF16)
        for n, field in enumerate((dq, dk, dv)):
            if n < 2:
                field = rotated(field, cos_t[...], left_t[...], right_t[...], -1.0)
            field = field.astype(BF16)
            tb[:, pl.ds(pl.multiple_of(n * 384 + pair * 128, 128), 128)] = field
            gvec[0:1, pl.ds(pl.multiple_of(5 * D + n * 384 + pair * 128, 128), 128)] = jnp.sum(
                field.astype(F32), axis=0, keepdims=True
            )
        return carry

    lax.fori_loop(0, 3, attend, 0)

    def units(i, carry):
        def at(begin):
            return pl.ds(pl.multiple_of(begin + i * 256, 128), 256)

        pre = nn(s2[...], w[:, at(INNER)]) + rowvec(pl.multiple_of(5 * D + 1152 + i * 256, 128), 256)
        phi = 0.5 * (1.0 + lax.erf(pre * (1.0 / math.sqrt(2.0))))
        act[:, at(0)] = (pre * phi).astype(BF16)
        slope = phi + pre * jnp.exp(-0.5 * pre * pre) * (1.0 / math.sqrt(2.0 * math.pi))
        back = (nn(up[...], w[:, at(OUTER)]) * slope).astype(BF16)
        ub[:, at(0)] = back
        gvec[0:1, at(5 * D + 1152)] = jnp.sum(back.astype(F32), axis=0, keepdims=True)
        return carry

    lax.fori_loop(0, 6, units, 0)

    def width_rows(i, carry):
        rows = pl.ds(pl.multiple_of(i * 256, 256), 256)

        def lanes(begin):
            return pl.ds(pl.multiple_of(begin + i * 256, 256), 256)

        outp[:, rows] += nt(ctx[...], w[rows, DENSE:INNER]) + nt(act[...], w[rows, OUTER : OUTER + 1536])
        second = nt(ub[...], w[rows, INNER:OUTER])
        first = nt(tb[...], w[rows, PROJ:SMALL])
        nbp[:, rows] = first * vec[0:1, lanes(0)] + second * vec[0:1, lanes(D)]
        normal = hat[:, rows]
        for n, term in enumerate((first * normal, second * normal, first, second)):
            gvec[0:1, lanes(n * D)] = jnp.sum(term, axis=0, keepdims=True)
        g[rows, PROJ:SMALL] = nn(s1t[rows, :], tb[...]).astype(BF16)
        g[rows, DENSE:INNER] = nn(upt[rows, :], ctx[...]).astype(BF16)
        g[rows, INNER:OUTER] = nn(s2t[rows, :], ub[...]).astype(BF16)
        g[rows, OUTER : OUTER + 1536] = nn(upt[rows, :], act[...]).astype(BF16)
        g[rows, OUTER + 1536 : COLS] = jnp.zeros((256, COLS - OUTER - 1536), BF16)
        return carry

    lax.fori_loop(0, 3, width_rows, 0)

    tile = jnp.zeros((64, 128), F32)
    for begin in range(0, VEC, D):
        width = min(D, VEC - begin)
        cols = slice(begin, begin + width)
        tile += nt((gvec[0:1, cols] * mask[:, cols].astype(F32)).astype(BF16), spread[:, cols])
    g[:, SMALL:DENSE] = nn(rows_at[...], tile.astype(BF16)).astype(BF16)

    side = lax.axis_index("tensor")
    own = pl.ds(pl.multiple_of(side * HALF_T, HALF_T), HALF_T)
    other = pl.ds(pl.multiple_of((1 - side) * HALF_T, HALF_T), HALF_T)
    residual = nn(x[other, :], perm[...]) + fb
    out_send[...] = (outp[other, :] - residual).astype(BF16)
    base_out[...] = outp[own, :]
    nb_send[...] = nbp[other, :].astype(BF16)
    nb_own[...] = nbp[own, :]
    hat_own[...] = hat[own, :]
    fac_own[...] = fac[own, :]
    up_own[...] = up[own, :]


def reduce_kernel(
    g, base_out, out_send, nb_own, nb_send, hat_own, fac_own, up_own, perm, pick_t,
    out, grad, small_out, rows_out,
    total, land, a1, a2, a3, a4, b1, b2, b3, b4, red, quad_send, quad_land, out_land, nb_land, small_land, small_mine,
    psend, precv, lsem, csend, crecv, rsend, rrecv, qsend, qrecv, esend, erecv,
):
    me = Place()
    enter(me)
    partner = me.dev(t=1 - me.t)
    sibling = me.dev(c=1 - me.c)
    waits = [
        remote(out_send, out_land, psend.at[0], precv.at[0], partner),
        remote(nb_send, nb_land, psend.at[1], precv.at[1], partner),
    ]
    axes = (("z", "y"), ("y", "z"))

    def block(ref, part, step, piece=None, core=None):
        begin, width = PART[part]
        if piece is not None:
            first, second = CUT[part][1:]
            begin, width = (begin, first) if piece == 0 else (begin + first, second)
        if core is not None:
            cols = pl.ds(pl.multiple_of(core * HALF + begin, 128), width)
        else:
            cols = pl.ds(begin, width)
        if axes[part][0] == "y":
            return ref.at[lax.rem(me.y + step, 4), :, :, cols]
        return ref.at[:, lax.rem(me.z + step, 4), :, cols]

    order = [(step, part) for step in (2, 1, 3, 0) for part in range(2)]
    pulls = {}
    for n, (step, part) in enumerate(order):
        local = pltpu.make_async_copy(block(g, part, step, core=me.c), block(total, part, step), lsem.at[n])
        local.start()
        copy = remote(
            block(g, part, step, core=1 - me.c), block(land, part, step), csend.at[n], crecv.at[n], sibling
        )
        pulls[step, part] = (local, copy)

    def add(dst, *terms):
        def body(i, carry):
            sum_ = dst[i].astype(F32)
            for term in terms:
                sum_ += term[i].astype(F32)
            dst[i] = sum_.astype(BF16)
            return carry

        lax.fori_loop(0, 4, body, 0)

    def join(step, part):
        local, copy = pulls[step, part]
        local.wait()
        copy.wait_recv()
        add(block(total, part, step), block(land, part, step))

    land1 = ((a1, a2, a3, a4), (b1, b2, b3, b4))
    copies = {}
    for part in range(2):
        join(2, part)
        for i, step in enumerate((1, 3)):
            copies[part, i] = remote(
                block(total, part, 2, i), land1[part][i], rsend.at[part, 0, i], rrecv.at[part, 0, i],
                me.ring(axes[part][0], step),
            )
    for part in range(2):
        for i, step in enumerate((1, 3)):
            join(step, part)
            copies[part, i].wait_recv()
            add(block(total, part, step, i), land1[part][i])
            copies[part, 2 + i] = remote(
                block(total, part, step), land1[part][2 + i], rsend.at[part, 0, 2 + i], rrecv.at[part, 0, 2 + i],
                me.ring(axes[part][0], step),
            )
    for part in range(2):
        join(0, part)
    for copy in waits:
        copy.wait()

    def finish(i, carry):
        rows = pl.ds(pl.multiple_of(i * 64, 64), 64)
        low = (base_out[rows, :] + out_land[rows, :].astype(F32)).astype(BF16)
        out[rows, :] = nt(low, perm[...]).astype(BF16)
        back = nb_own[rows, :] + nb_land[rows, :].astype(F32)
        normal = hat_own[rows, :]
        value = up_own[rows, :].astype(F32) + fac_own[rows, 0:1] * (
            back
            - jnp.mean(back, axis=-1, keepdims=True)
            - normal * jnp.mean(back * normal, axis=-1, keepdims=True)
        )
        grad[rows, :] = nt(value.astype(BF16), perm[...]).astype(BF16)
        return carry

    lax.fori_loop(0, 4, finish, 0)

    for part in range(2):
        for i in range(2):
            copies[part, 2 + i].wait_recv()
        add(block(total, part, 0), land1[part][2], land1[part][3])
    for copy in copies.values():
        copy.wait_send()

    def piece_of(part, step, piece=None):
        begin, width = PART[part]
        if piece is not None:
            first, second = CUT[part][1:]
            begin, width = (begin, first) if piece == 0 else (begin + first, second)
        cols = pl.ds(begin, width)
        if axes[part][1] == "y":
            return total.at[lax.rem(me.y + step, 4), me.z, :, cols]
        return total.at[me.y, lax.rem(me.z + step, 4), :, cols]

    land2 = []
    for part in range(2):
        begin, width = PART[part]
        first, second = CUT[part][1:]
        land2.append(
            (
                red.at[0, :, pl.ds(begin, first)],
                red.at[0, :, pl.ds(begin + first, second)],
                red.at[1, :, pl.ds(begin, width)],
                red.at[2, :, pl.ds(begin, width)],
            )
        )
    more = {}
    for part in range(2):
        for i, step in enumerate((1, 3)):
            more[part, i] = remote(
                piece_of(part, 2, i), land2[part][i], rsend.at[part, 1, i], rrecv.at[part, 1, i],
                me.ring(axes[part][1], step),
            )
    for part in range(2):
        for i, step in enumerate((1, 3)):
            more[part, i].wait_recv()
            piece = piece_of(part, step, i)
            piece[...] = (piece[...].astype(F32) + land2[part][i][...].astype(F32)).astype(BF16)
            more[part, 2 + i] = remote(
                piece_of(part, step), land2[part][2 + i], rsend.at[part, 1, 2 + i], rrecv.at[part, 1, 2 + i],
                me.ring(axes[part][1], step),
            )
    for part in range(2):
        begin, width = PART[part]
        for i in range(2):
            more[part, 2 + i].wait_recv()
        sum_ = (
            total[me.y, me.z, :, pl.ds(begin, width)].astype(F32)
            + land2[part][2][...].astype(F32)
            + land2[part][3][...].astype(F32)
        )
        quad_send[:, :, pl.ds(begin, width)] = (
            nn(pick_t[...], sum_.astype(BF16)).astype(BF16).reshape(4, PAD, width)
        )
    quads = []
    for r in (1, 2, 3):
        device, xh, c = me.quad(r)
        quads.append(remote(quad_send.at[xh * 2 + c], quad_land.at[me.slot], qsend.at[r], qrecv.at[r], device))
    quad_land[me.slot] = quad_send[me.slot]
    for copy in quads:
        copy.wait_recv()
    for c in range(2):
        rows_out[:, c * HALF : (c + 1) * HALF] = quad_land[c].astype(F32) + quad_land[2 + c].astype(F32)
    small_mine[...] = rows_out[:, SMALL:DENSE]
    last = remote(small_mine, small_land, esend, erecv, partner)
    for copy in more.values():
        copy.wait_send()
    for copy in quads:
        copy.wait_send()
    for local, copy in pulls.values():
        copy.wait_send()
    last.wait()
    lane = lax.broadcasted_iota(jnp.int32, (PAD, 128), 1)
    small_out[...] = small_mine[...] + jnp.where(lane < 4 * OWN, small_land[...], 0.0)


def turn_tables(starts):
    places = (jnp.arange(T, dtype=jnp.int32) - starts).astype(F32)
    lane = jnp.arange(128, dtype=jnp.int32) % HD
    freqs = jnp.exp((lane % 8).astype(F32) * (-2.0 * math.log(10000.0) / ROT))
    turns = places[:, None] * freqs[None, :]
    cosine, sine = jnp.cos(turns), jnp.sin(turns)
    return (
        jnp.where(lane < ROT, cosine, 1.0),
        jnp.where(lane < 8, -sine, 0.0),
        jnp.where((lane >= 8) & (lane < ROT), sine, 0.0),
    )


def local(
    layer_input, segment_starts, norm_gains, norm_shifts, projection, triple_bias, dense_weight, inner_weight,
    unit_bias, outer_weight, final_bias, cotangent,
):
    perm, spread, mask, rows_at, rows_of, pick, pick_t = [jnp.asarray(m) for m in order_tables()]
    small = jnp.concatenate(
        [norm_gains.reshape(-1), norm_shifts.reshape(-1), final_bias, triple_bias.reshape(-1), unit_bias]
    )
    small = jnp.pad(small[None, :], ((0, OWN - 1), (0, 128 - small.shape[0])))
    mine = jnp.concatenate(
        [
            projection.reshape(OWN, 1152),
            small,
            dense_weight.T,
            inner_weight,
            outer_weight.T,
            jnp.zeros((OWN, 128), BF16),
        ],
        axis=1,
    )
    mine = jnp.pad(mine, ((0, PAD - OWN), (0, 0)))
    vm = pl.BlockSpec(memory_space=pltpu.VMEM)
    anywhere = pl.BlockSpec(memory_space=pl.ANY)
    dma = pltpu.SemaphoreType.DMA
    struct = jax.ShapeDtypeStruct

    w, xall, cotall = pl.pallas_call(
        gather_kernel,
        out_shape=(struct((Y, Z, BLK, COLS), BF16), struct((T, D), BF16), struct((T, D), BF16)),
        in_specs=[vm, anywhere, anywhere, vm],
        out_specs=(anywhere,) * 3,
        scratch_shapes=[
            pltpu.VMEM((4, PAD, HALF), BF16),
            pltpu.VMEM((BLK, HALF), BF16),
            dma((4,)), dma((4,)), dma((2, 2, 4)), dma((2, 2, 4)), dma((13,)), dma((13,)), dma((2,)), dma((2,)), dma((3,)),
        ],
        compiler_params=pltpu.CompilerParams(collective_id=0, has_side_effects=True),
        name="gather",
    )(mine, layer_input, cotangent, pick)

    tables = turn_tables(segment_starts)
    start_col = jnp.broadcast_to(segment_starts[:, None], (T, 128))
    start_row = jnp.broadcast_to(segment_starts[None, :], (8, T))
    rows = lambda kind, n=D: struct((HALF_T, n), kind)
    vmem = pltpu.VMEM
    g, base_out, out_send, nb_own, nb_send, hat_own, fac_own, up_own = pl.pallas_call(
        compute_kernel,
        out_shape=(
            struct((D, COLS), BF16), rows(F32), rows(BF16), rows(F32), rows(BF16), rows(F32), rows(F32, 128), rows(BF16),
        ),
        in_specs=[vm] * 13,
        out_specs=(vm,) * 8,
        scratch_shapes=[vmem((T, D), BF16)] * 3
        + [vmem((D, T), BF16)] * 3
        + [vmem((T, D), F32), vmem((T, 128), F32)]
        + [vmem((T, 384), BF16)] * 5
        + [vmem((T, 1152), BF16), vmem((T, 1536), BF16), vmem((T, 1536), BF16), vmem((T, D), F32), vmem((T, D), F32)]
        + [vmem((8, VEC), F32)] * 2,
        compiler_params=pltpu.CompilerParams(vmem_limit_bytes=VMEM_LIMIT),
        name="layer",
    )(
        w.reshape(D, COLS), xall, cotall, perm, spread, mask, rows_at, rows_of, *tables, start_col, start_row
    )

    out, grad, small_grad, rows_grad = pl.pallas_call(
        reduce_kernel,
        out_shape=(rows(BF16), rows(BF16), struct((PAD, 128), F32), struct((PAD, COLS), F32)),
        in_specs=[anywhere] + [vm] * 9,
        out_specs=(vm,) * 4,
        scratch_shapes=[
            vmem((Y, Z, BLK, HALF), BF16), vmem((Y, Z, BLK, HALF), BF16),
            vmem((4, BLK, 640), BF16), vmem((4, BLK, 640), BF16), vmem((4, BLK, 1280), BF16), vmem((4, BLK, 1280), BF16),
            vmem((4, BLK, 640), BF16), vmem((4, BLK, 512), BF16), vmem((4, BLK, 1152), BF16), vmem((4, BLK, 1152), BF16),
            vmem((3, BLK, HALF), BF16), vmem((4, PAD, HALF), BF16), vmem((4, PAD, HALF), BF16),
            vmem((HALF_T, D), BF16), vmem((HALF_T, D), BF16), vmem((PAD, 128), F32), vmem((PAD, 128), F32),
            dma((2,)), dma((2,)), dma((8,)), dma((8,)), dma((8,)), dma((2, 2, 4)), dma((2, 2, 4)), dma((4,)), dma((4,)),
            dma, dma,
        ],
        compiler_params=pltpu.CompilerParams(collective_id=1, has_side_effects=True, vmem_limit_bytes=VMEM_LIMIT),
        name="reduce",
    )(
        g.reshape(Y, Z, BLK, COLS), base_out, out_send, nb_own, nb_send, hat_own, fac_own, up_own, perm, pick_t
    )

    vals = small_grad[0]
    side = lax.axis_index("tensor")

    def six(field):
        return lax.dynamic_slice_in_dim(field, side * 6, 6, axis=field.ndim - 1)

    own = rows_grad[:OWN]
    return (
        out,
        grad,
        six(vals[0:24].reshape(2, OWN)),
        six(vals[24:48].reshape(2, OWN)),
        own[:, PROJ:SMALL].reshape(OWN, 3, 384),
        vals[OFF_TB:OFF_UB].reshape(3, 6),
        own[:, DENSE:INNER].T,
        own[:, INNER:OUTER],
        vals[OFF_UB : OFF_UB + 24],
        own[:, OUTER : OUTER + 1536].T,
        six(vals[48:60]),
    )


def solution(mesh):
    placed = (
        P(("dp", "tensor"), None),
        P("dp"),
        P(None, "dp"),
        P(None, "dp"),
        P("dp", None, "tensor"),
        P(None, ("tensor", "dp")),
        P("tensor", "dp"),
        P("dp", "tensor"),
        P(("tensor", "dp")),
        P("tensor", "dp"),
        P("dp"),
        P(("dp", "tensor"), None),
    )
    return jax.shard_map(
        local,
        mesh=mesh,
        in_specs=placed,
        out_specs=(
            P(("dp", "tensor"), None),
            P(("dp", "tensor"), None),
            P(None, ("dp", "tensor")),
            P(None, ("dp", "tensor")),
            P("dp", None, "tensor"),
            P(None, ("tensor", "dp")),
            P("tensor", "dp"),
            P("dp", "tensor"),
            P(("tensor", "dp")),
            P("tensor", "dp"),
            P(("dp", "tensor")),
        ),
        check_vma=False,
    )
```

time: 1470 us -> 161 us (0.11)
  blocking collectives: 1160 us -> 0 us
  Pallas kernels: 0 us -> 133 us
  starting transfers between devices: 132 us -> 0 us
  matrix products: 56.4 us -> 0 us
  local copies, waits for them, and re-layouts: 73.7 us -> 23.9 us
  between operations: 20.2 us -> 0.7 us
    unnamed x4 -> x0, blocking collectives: 757 us -> none
    all_gather x7 -> x0, blocking collectives: 401 us -> none  [the longest x1 101 us: local(): lax.all_gather(dense_weight, 'dp', axis=1, tiled=True)]
    pallas_call x0 -> x3, Pallas kernels: none -> 133 us  [the longest x1 46.9 us: local(): pl.pallas_call(gather_kernel, out_shape=(struct((Y, Z, BLK, COLS), BF16),...]
    unnamed x49 -> x0, starting transfers between devices: 132 us -> none
    unnamed x166 -> x9, local copies, waits for them, and re-layouts: 69.9 us -> 6.66 us
    dot_general x18 -> x0, matrix products: 56.4 us -> none  [product(): return jnp.einsum(form, left, right, preferred_element_type=jnp.float32)]
  transfers between devices with their start and end apart: 56 -> 0, of which waited for: 0 -> 0; matrix products, arithmetic and copies ran while one was open for 22% -> 0% of each run, Pallas kernels for 0% -> 0%
where the time goes in v1:
time: 161 us; the launch traced here: 160 us
  Pallas kernels  133 us (83%)
  local copies, waits for them, and re-layouts  23.9 us (15%)
  other arithmetic  2.61 us (2%)
    pallas_call x1, Pallas kernels, local(): pl.pallas_call(gather_kernel, out_shape=(struct((Y, Z, BLK, COLS), BF16),...  46.9 us
    pallas_call x1, Pallas kernels, local(): pl.pallas_call(reduce_kernel, out_shape=(rows(BF16), rows(BF16), struct((...  44.7 us
    pallas_call x1, Pallas kernels, local(): pl.pallas_call(compute_kernel, out_shape=(struct((D, COLS), BF16), rows(F...  41.1 us
    unnamed x9, local copies, waits for them, and re-layouts  6.66 us

profile of v1, /device:TPU:1, one launch (start us, length us, event | category | flops | bytes accessed | tf_op | source)
XLA Modules:
  0.0 159.9 jit_solution(9951594202689207386)
XLA Ops:
  0.7 0.7 subtract_convert_fusion
  1.4 1.9 %fusion = (f32[512,128]{1,0:T(8,128)}, f32[512,128]{1,0:T(8,128)}, f32[512,128]{1,0:T(8,128)}) fusion(f32[128]{0:T(128)S(1)} %fusion.7, f32[512]{0:T(512)S(1)} %subtract_convert_fusion, pred[128]{0:T(512)(128)(4,1)S(1)} %get-tuple-element.49, pred[128]{0:T(512)(128)(4,1)S(1)} %get-tuple-element.50, pred[128]{0:T(512)(128)(4,1)S(1)} %broadcast_compare_fusion.1), kind=kLoop, calls=%fused_computation.2 | loop fusion | flops 327680 | bytes 789376 | tf_op jit(solution)/shard_map/jit(_where)/select_n | solution.py:571
  3.3 0.8 pad.10
  4.1 0.7 reshape.88
  4.8 0.7 reshape.89
  5.6 0.8 reshape.90
  6.3 1.4 concatenate.6
  7.8 0.7 constant_dynamic-update-slice_fusion.2
  8.5 0.8 constant_dynamic-update-slice_fusion.1
  9.3 0.8 bitcast_dynamic-update-slice_fusion
  10.1 0.7 pad.9.mine
  10.8 46.9 %gather.1 = (bf16[4,4,48,4864]{3,2,1,0:T(8,128)(2,1)}, bf16[512,768]{1,0:T(8,128)(2,1)}, bf16[512,768]{1,0:T(8,128)(2,1)}) custom-call(bf16[16,4864]{1,0:T(8,128)(2,1)} %pad.9.mine, bf16[256,768]{1,0:T(8,128)(2,1)} %x.5, bf16[256,768]{1,0:T(8,128)(2,1)} %cot.1, bf16[48,64]{1,0:T(8,128)(2,1)} %constant.71.clone.pick), custom_call_target="tpu_custom_call" | custom-call | tf_op jit(solution)/shard_map/gather/pallas_call | solution.py:601
  57.6 1.5 broadcast_in_dim.45.start_col
  59.2 1.3 broadcast_in_dim.46.start_row
  60.4 41.1 %layer.1 = (bf16[768,4864]{1,0:T(8,128)(2,1)}, f32[256,768]{1,0:T(8,128)}, bf16[256,768]{1,0:T(8,128)(2,1)}, f32[256,768]{1,0:T(8,128)}, bf16[256,768]{1,0:T(8,1...) custom-call(bf16[768,4864]{1,0:T(8,128)(2,1)} %bitcast.19, ...), custom_call_target="tpu_custom_call" | custom-call | tf_op jit(solution)/shard_map/layer/pallas_call | solution.py:620
  101.6 44.7 %reduce.13 = (bf16[256,768]{1,0:T(8,128)(2,1)}, bf16[256,768]{1,0:T(8,128)(2,1)}, f32[16,128]{1,0:T(8,128)}, f32[16,4864]{1,0:T(8,128)}) custom-call(bf16[4,4,48,4864]{3,2,1,0:T(8,128)(2,1)} %bitcast.18, f32[256,768]{1,0:T(8,128)} %get-tuple-element.30.base_out, bf16[256,768]{1,0:T(8,128)(2,1)} %get-tuple-element.31.out_send, ...), custom_call_target="tpu_custom_call" | custom-call | tf_op jit(solution)/shard_map/reduce/pallas_call | solution.py:639
  146.3 1.6 %slice_bitcast_fusion = (f32[1536,12]{0,1:T(8,128)}, f32[12,1536]{1,0:T(8,128)}) fusion(f32[16,4864]{1,0:T(8,128)} %get-tuple-element.40), kind=kLoop, calls=%fused_computation.6 | loop fusion | bytes 294912 | tf_op jit(solution)/shard_map/transpose | solution.py:676
  148.0 0.9 slice.47
  149.5 1.3 slice_bitcast_fusion.1
  150.8 1.4 slice_reduce_fusion.1
  153.7 0.7 slice.54
  155.0 0.8 slice_reduce_fusion
  156.4 1.8 %copy.38 = bf16[256,768]{1,0:T(8,128)(2,1)} copy(bf16[256,768]{1,0:T(8,128)(2,1)} %get-tuple-element.62) | data formatting | bytes 786432
  158.2 1.8 %copy.39 = bf16[256,768]{1,0:T(8,128)(2,1)} copy(bf16[256,768]{1,0:T(8,128)(2,1)} %get-tuple-element.63) | data formatting | bytes 786432
  (14 shorter events, 3.4 us)

commit v2 on v1

v2 whole, which is shorter than its diff:
```python
import math

import jax
import jax.numpy as jnp
import numpy as np
from jax import lax
from jax.experimental import pallas as pl
from jax.experimental.pallas import tpu as pltpu
from jax.sharding import PartitionSpec as P

MESH = pl.DeviceIdType.MESH
F32, BF16 = jnp.float32, jnp.bfloat16

D, HD, ROT = 768, 64, 16
T, HALF_T = 512, 256
EPSILON = 1e-05
Y, XH, Z, CORE = 4, 2, 4, 2
OWN = 12
PAD = 16
BLK = OWN * XH * CORE
COLS, WIDE = 4864, 2432
W_SMALL, W_DENSE, W_UNITS = 1152, 1280, (1792, 3328)
G_DENSE, G_INNER, G_OUTER, G_SMALL = 1152, (1536, 3072), (2304, 3968), 3840
EVEN = ((0, 384), (384, 384))
UNEVEN = ((0, 512), (512, 384))
W_GROUPS = ((0, 896, UNEVEN, 0), (1792, 768, EVEN, 896), (3328, 768, EVEN, 1664))
G_GROUPS = ((0, 768, EVEN, 0), (1536, 768, EVEN, 768), (3072, 896, UNEVEN, 1536))
VEC = 5 * D + 3 * 384 + 1536
OFF_TB, OFF_UB = 5 * OWN, 5 * OWN + 18
VMEM_LIMIT = 56 * 1024 * 1024


def order_tables():
    j = np.arange(64)
    c, xh, z, y = j % 2, (j // 2) % 2, (j // 4) % 4, j // 16
    dp = ((y * 2 + xh) * 4 + z) * 2 + c
    at = (12 * dp[:, None] + np.arange(12)[None, :]).reshape(-1)
    perm = np.zeros((D, D), np.float32)
    perm[at, np.arange(D)] = 1
    spread = np.zeros((128, VEC), np.float32)
    mask = np.zeros((64, VEC), np.float32)
    col = np.arange(D)
    for v in range(5):
        spread[v * 12 + col % 12, v * D + col] = 1
        mask[col // 12, v * D + col] = 1
    back = np.argsort(dp)
    col = np.arange(384)
    for k in range(3):
        spread[OFF_TB + 6 * k + col % 6, 5 * D + 384 * k + col] = 1
        mask[back[col // 6], 5 * D + 384 * k + col] = 1
    col = np.arange(1536)
    spread[OFF_UB + col % 24, 5 * D + 1152 + col] = 1
    mask[back[col // 24], 5 * D + 1152 + col] = 1
    rows = np.zeros((D, 64), np.float32)
    rows[12 * j, j] = 1
    pick = np.zeros((BLK, 64), np.float32)
    r = np.arange(BLK)
    pick[r, 16 * (r // 12) + r % 12] = 1
    return [m.astype(jnp.bfloat16) for m in (perm, spread, mask, rows, np.ascontiguousarray(rows.T), pick, np.ascontiguousarray(pick.T))]


def nn(a, b):
    return lax.dot_general(a, b, (((1,), (0,)), ((), ())), preferred_element_type=F32)


def nt(a, b):
    return lax.dot_general(a, b, (((1,), (1,)), ((), ())), preferred_element_type=F32)


def tn(a, b):
    return lax.dot_general(a, b, (((0,), (0,)), ((), ())), preferred_element_type=F32)


class Place:
    def __init__(self):
        dp = lax.axis_index("dp")
        self.t = lax.axis_index("tensor")
        self.c = lax.rem(dp, 2)
        self.z = lax.rem(lax.div(dp, 2), 4)
        self.xh = lax.rem(lax.div(dp, 8), 2)
        self.y = lax.div(dp, 16)
        self.slot = self.xh * 2 + self.c

    def dev(self, y=None, xh=None, z=None, c=None, t=None):
        y = self.y if y is None else y
        xh = self.xh if xh is None else xh
        z = self.z if z is None else z
        c = self.c if c is None else c
        t = self.t if t is None else t
        return (((y * 2 + xh) * 4 + z) * 2 + c, t)

    def ring(self, axis, step):
        at = lax.rem((self.y if axis == "y" else self.z) + step, 4)
        return self.dev(y=at) if axis == "y" else self.dev(z=at)

    def quad(self, r):
        c = 1 - self.c if r & 1 else self.c
        xh = 1 - self.xh if r & 2 else self.xh
        return self.dev(xh=xh, c=c), xh, c

    def peers(self):
        out = [self.quad(r)[0] for r in (1, 2, 3)]
        for axis in ("y", "z"):
            out += [self.ring(axis, step) for step in (1, 2, 3)]
        return out + [self.dev(t=1 - self.t)]


def enter(place):
    barrier = pltpu.get_barrier_semaphore()
    peers = place.peers()
    for peer in peers:
        pl.semaphore_signal(barrier, inc=1, device_id=peer, device_id_type=MESH)
    pl.semaphore_wait(barrier, len(peers))


class Copy:
    def __init__(self, parts):
        self.parts = parts
        self.make().start()

    def make(self):
        src, dst, send, recv, device = self.parts()
        return pltpu.make_async_remote_copy(
            src_ref=src, dst_ref=dst, send_sem=send, recv_sem=recv, device_id=device, device_id_type=MESH
        )

    def wait_recv(self):
        self.make().wait_recv()

    def wait_send(self):
        self.make().wait_send()


def span(begin, width):
    return pl.ds(begin if isinstance(begin, int) else pl.multiple_of(begin, 128), width)


def cut(part, width):
    first = 256 if part == 0 or width == 512 else 128
    return ((0, first), (first, width - first))


class Gather:
    axes = (("y", "z"), ("z", "y"))

    def __init__(self, me, w, sems):
        self.me, self.w = me, w
        self.p0s, self.p0r, self.p1s, self.p1r, self.ss, self.sr = sems
        self.sibling = me.dev(c=1 - me.c)
        self.first, self.second, self.shared = {}, {}, {}

    def cols(self, group, part, piece=None):
        base, half, parts, _ = W_GROUPS[group]
        begin, width = parts[part]
        if piece is not None:
            more, width = cut(part, width)[piece]
            begin += more
        return span(self.me.c * half + (base + begin), width)

    def unit(self, group, part, step, piece=None):
        cols = self.cols(group, part, piece)
        if self.axes[part][1] == "y":
            return self.w.at[lax.rem(self.me.y + step, 4), :, :, cols]
        return self.w.at[:, lax.rem(self.me.z + step, 4), :, cols]

    def share(self, group, part, step):
        def parts():
            ref = self.unit(group, part, step)
            return ref, ref, self.ss.at[group, part, step], self.sr.at[group, part, step], self.sibling

        self.shared[group, part, step] = Copy(parts)

    def start(self, group):
        me = self.me
        for part in range(2):
            for step in (2, 1, 3):

                def parts(part=part, step=step):
                    at = (group, part, step - 1)
                    ref = self.w.at[me.y, me.z, :, self.cols(group, part)]
                    return ref, ref, self.p0s.at[at], self.p0r.at[at], me.ring(self.axes[part][0], step)

                self.first[group, part, step - 1] = Copy(parts)

    def onward(self, group, part, origin, piece, sem, step):
        def parts():
            ref, at = self.unit(group, part, origin, piece), (group, part, sem)
            return ref, ref, self.p1s.at[at], self.p1r.at[at], self.me.ring(self.axes[part][1], step)

        self.second[group, part, sem] = Copy(parts)

    def turn(self, group):
        for part in range(2):
            for step in (1, 3, 2):
                self.first[group, part, step - 1].wait_recv()
            for i, step in enumerate((1, 3)):
                self.onward(group, part, 0, None, i, step)
            self.share(group, part, 0)

    def forward(self, group):
        for part in range(2):
            for i, step in enumerate((1, 3)):
                self.second[group, part, i].wait_recv()
                self.onward(group, part, 4 - step, i, 2 + i, step)
                self.share(group, part, 4 - step)

    def finish(self, group):
        for part in range(2):
            for i in range(2):
                self.second[group, part, 2 + i].wait_recv()
            self.share(group, part, 2)

    def done(self, group):
        for part in range(2):
            for step in range(4):
                self.shared[group, part, step].wait_recv()

    def sent(self):
        for copies in (self.first, self.second, self.shared):
            for copy in copies.values():
                copy.wait_send()


class Reduce:
    axes = (("z", "y"), ("y", "z"))

    def __init__(self, me, g, land, ring1, ring2, red, sems):
        self.me, self.g, self.land, self.ring1, self.ring2, self.red = me, g, land, ring1, ring2, red
        self.cs, self.cr, self.p0s, self.p0r, self.p1s, self.p1r = sems
        self.sibling = me.dev(c=1 - me.c)
        self.pulled, self.first, self.second = {}, {}, {}

    def place(self, group, part, piece=None):
        _, _, parts, at = G_GROUPS[group]
        begin, width = parts[part]
        if piece is not None:
            more, width = cut(part, width)[piece]
            begin += more
        return begin, at + begin, width

    def unit(self, group, part, step, piece=None, core=None):
        base, half, _, _ = G_GROUPS[group]
        begin, _, width = self.place(group, part, piece)
        cols = span((self.me.c if core is None else core) * half + (base + begin), width)
        return self.of(self.g, part, step, cols)

    def of(self, ref, part, step, cols):
        if self.axes[part][0] == "y":
            return ref.at[lax.rem(self.me.y + step, 4), :, :, cols]
        return ref.at[:, lax.rem(self.me.z + step, 4), :, cols]

    def landed(self, group, part, step):
        _, at, width = self.place(group, part)
        return self.of(self.land, part, step, span(at, width))

    def add(self, dst, *terms):
        def body(i, carry):
            total = dst[i].astype(F32)
            for term in terms:
                total += term[i].astype(F32)
            dst[i] = total.astype(BF16)
            return carry

        lax.fori_loop(0, 4, body, 0)

    def pull(self, group, part):
        for step in (2, 1, 3, 0):

            def parts(step=step):
                at = (group, part, step)
                src = self.unit(group, part, step, core=1 - self.me.c)
                return src, self.landed(group, part, step), self.cs.at[at], self.cr.at[at], self.sibling

            self.pulled[group, part, step] = Copy(parts)

    def join(self, group, part, step):
        self.pulled[group, part, step].wait_recv()
        self.add(self.unit(group, part, step), self.landed(group, part, step))

    def piece1(self, group, part, i):
        _, at, width = self.place(group, part, i)
        return self.ring1.at[:, :, span(at, width)]

    def start(self, group):
        for part in range(2):
            self.join(group, part, 2)
            for i, step in enumerate((1, 3)):

                def parts(part=part, i=i, step=step):
                    at = (group, part, i)
                    src, dst = self.unit(group, part, 2, i), self.piece1(group, part, i)
                    return src, dst, self.p0s.at[at], self.p0r.at[at], self.me.ring(self.axes[part][0], step)

                self.first[group, part, i] = Copy(parts)

    def whole2(self, group, part, i):
        _, at, width = self.place(group, part)
        return self.ring2.at[i, :, :, span(at, width)]

    def turn(self, group):
        for part in range(2):
            for i, step in enumerate((1, 3)):
                self.join(group, part, step)
                self.first[group, part, i].wait_recv()
                self.add(self.unit(group, part, step, i), self.piece1(group, part, i))

                def parts(part=part, i=i, step=step):
                    at = (group, part, 2 + i)
                    src, dst = self.unit(group, part, step), self.whole2(group, part, i)
                    return src, dst, self.p0s.at[at], self.p0r.at[at], self.me.ring(self.axes[part][0], step)

                self.first[group, part, 2 + i] = Copy(parts)

    def across(self, group, part, step):
        me = self.me
        base, half, _, _ = G_GROUPS[group]
        begin, _, width = self.place(group, part)
        cols = span(me.c * half + (base + begin), width)
        if self.axes[part][1] == "y":
            return self.g.at[lax.rem(me.y + step, 4), me.z, :, cols]
        return self.g.at[me.y, lax.rem(me.z + step, 4), :, cols]

    def finish(self, group):
        for part in range(2):
            self.join(group, part, 0)
            for i in range(2):
                self.first[group, part, 2 + i].wait_recv()
            self.add(self.unit(group, part, 0), self.whole2(group, part, 0), self.whole2(group, part, 1))
            for step in (2, 1, 3):

                def parts(part=part, step=step):
                    _, at, width = self.place(group, part)
                    sem = (group, part, step - 1)
                    src, dst = self.across(group, part, step), self.red.at[step - 1, :, span(at, width)]
                    return src, dst, self.p1s.at[sem], self.p1r.at[sem], self.me.ring(self.axes[part][1], step)

                self.second[group, part, step - 1] = Copy(parts)

    def done(self, group, pick_t, quad):
        for part in range(2):
            _, at, width = self.place(group, part)
            total = self.across(group, part, 0)[...].astype(F32)
            for step in (1, 3, 2):
                self.second[group, part, step - 1].wait_recv()
                total += self.red[step - 1, :, at : at + width].astype(F32)
            quad[:, :, at : at + width] = nn(pick_t[...], total.astype(BF16)).astype(BF16).reshape(4, PAD, width)

    def sent(self):
        for copies in (self.pulled, self.first, self.second):
            for copy in copies.values():
                copy.wait_send()


def rotated(field, cosine, left, right, sign):
    n = field.shape[1]
    return field * cosine + sign * (pltpu.roll(field, n - 8, 1) * left + pltpu.roll(field, 8, 1) * right)


def kernel(
    mine, x, cot, perm, spread, mask, rows_at, rows_of, pick, pick_t, cos_t, left_t, right_t, start_col, start_row,
    out, grad, small_out, rows_out,
    w, g, land, ring1, ring2, red, quad_in, quad_out, quad_land, x_land, cot_land, out_send, out_land, nb_send, nb_land,
    small_mine, small_land,
    s1, s2, up, s1t, s2t, upt, hat, fac, q, k, v, cb, ctx, tb, act, ub, outp, sec, nbp, vec, gvec,
    ap0s, ap0r, ap1s, ap1r, ass, asr, rcs, rcr, rp0s, rp0r, rp1s, rp1r, qs, qr, ts, tr, es, er,
):
    me = Place()
    enter(me)
    partner = me.dev(t=1 - me.t)
    gather = Gather(me, w, (ap0s, ap0r, ap1s, ap1r, ass, asr))
    reduce = Reduce(me, g, land, ring1, ring2, red, (rcs, rcr, rp0s, rp0r, rp1s, rp1r))
    quads, swaps = [], []
    for r in (1, 2, 3):

        def parts(r=r):
            device, _, c = me.quad(r)
            return mine.at[c], quad_in.at[me.slot], qs.at[0, r], qr.at[0, r], device

        quads.append(Copy(parts))
    for i, (src, dst) in enumerate(((x, x_land), (cot, cot_land))):
        swaps.append(Copy(lambda src=src, dst=dst, i=i: (src, dst, ts.at[i], tr.at[i], partner)))
    quad_in[me.slot] = mine[me.c]
    gvec[...] = jnp.zeros_like(gvec)
    for copy in quads:
        copy.wait_recv()
    block = nn(pick[...], quad_in[...].reshape(64, WIDE)).astype(BF16)
    for base, half, _, at in W_GROUPS:
        w[me.y, me.z, :, span(me.c * half + base, half)] = block[:, at : at + half]
    gather.start(0)

    def norm_rows(x_ref, cot_ref, first_row):
        def body(i, carry):
            src = pl.ds(pl.multiple_of(i * 128, 128), 128)
            rows = pl.ds(pl.multiple_of(first_row + i * 128, 128), 128)
            field = nn(x_ref[src, :], perm[...])
            center = jnp.mean(field, axis=-1, keepdims=True)
            centred = field - center
            factor = lax.rsqrt(jnp.mean(centred * centred, axis=-1, keepdims=True) + EPSILON)
            hat[rows, :] = centred * factor
            fac[rows, :] = jnp.broadcast_to(factor, (128, 128))
            upstream = nn(cot_ref[src, :], perm[...])
            up[rows, :] = upstream.astype(BF16)
            upt[:, rows] = upstream.astype(BF16).T
            gvec[0:1, 4 * D : 5 * D] += jnp.sum(upstream, axis=0, keepdims=True)
            return carry

        lax.fori_loop(0, 2, body, 0)

    norm_rows(x, cot, me.t * HALF_T)
    gather.turn(0)
    gather.start(1)
    for copy in swaps:
        copy.wait_recv()
    norm_rows(x_land, cot_land, (1 - me.t) * HALF_T)
    gather.forward(0)
    gather.finish(0)
    gather.turn(1)
    gather.start(2)
    gather.done(0)

    def wcols(begin, width):
        return w[:, :, :, span(begin, width)].reshape(D, width)

    def wrows(i, begin, width):
        return w[2 * i : 2 * i + 2, :, :, begin : begin + width].reshape(384, width)

    def put(i, begin, value):
        width = value.shape[1]
        g[2 * i : 2 * i + 2, :, :, begin : begin + width] = value.astype(BF16).reshape(2, Z, BLK, width)

    small = nn(rows_of[...], wcols(W_SMALL, 128)).astype(BF16)
    for begin in range(0, VEC, D):
        width = min(D, VEC - begin)
        cols = slice(begin, begin + width)
        picked = nn(small, spread[:, cols]) * mask[:, cols].astype(F32)
        vec[:, cols] = jnp.broadcast_to(jnp.sum(picked, axis=0, keepdims=True), (8, width))

    def rowvec(begin, width):
        return vec[0:1, span(begin, width)]

    g0, g1, h0, h1, fb = (vec[0:1, i * D : (i + 1) * D] for i in range(5))

    def scale_rows(i, carry):
        rows = pl.ds(pl.multiple_of(i * 128, 128), 128)
        normal = hat[rows, :]
        first = (normal * g0 + h0).astype(BF16)
        second = (normal * g1 + h1).astype(BF16)
        s1[rows, :] = first
        s2[rows, :] = second
        s1t[:, rows] = first.T
        s2t[:, rows] = second.T
        return carry

    lax.fori_loop(0, 4, scale_rows, 0)

    def heads_in(i, carry):
        cols = span(i * 128, 128)
        for n, ref in enumerate((q, k, v)):
            field = nn(s1[...], wcols(n * 384 + i * 128, 128)) + rowvec(5 * D + n * 384 + i * 128, 128)
            if n < 2:
                field = rotated(field, cos_t[...], left_t[...], right_t[...], 1.0)
            ref[:, cols] = field.astype(BF16)
        cb[:, cols] = nn(up[...], wcols(W_DENSE + i * 128, 128)).astype(BF16)
        return carry

    lax.fori_loop(0, 3, heads_in, 0)
    gather.forward(1)

    scale = 1.0 / math.sqrt(HD)

    def attend(pair, carry):
        cols = span(pair * 128, 128)
        halves = []
        for head in range(2):
            inside = (lax.broadcasted_iota(jnp.int32, (1, 128), 1) // HD) == head
            grads_k, grads_v, outs, grads_q = [], [], [], []
            for block in range(2):
                begin, n = block * HALF_T, (block + 1) * HALF_T
                rows = slice(begin, begin + HALF_T)
                kk, vv = k[0:n, cols], v[0:n, cols]
                qq = jnp.where(inside, q[rows, cols], 0).astype(BF16)
                cc = jnp.where(inside, cb[rows, cols], 0).astype(BF16)
                place_t = begin + lax.broadcasted_iota(jnp.int32, (HALF_T, n), 0)
                place_s = lax.broadcasted_iota(jnp.int32, (HALF_T, n), 1)
                allowed = (start_col[rows, 0:1] == start_row[0:1, 0:n]) & (place_s <= place_t)
                scores = jnp.where(allowed, nt(qq, kk) * scale, -1e30)
                powers = jnp.exp(scores - jnp.max(scores, axis=-1, keepdims=True))
                probs = powers / jnp.sum(powers, axis=-1, keepdims=True)
                low = probs.astype(BF16)
                outs.append(nn(low, vv))
                back = nt(cc, vv)
                inner = jnp.sum(probs * back, axis=-1, keepdims=True)
                ds = (probs * (back - inner)).astype(BF16)
                grads_q.append(nn(ds, kk) * scale)
                grads_k.append(tn(ds, qq) * scale)
                grads_v.append(tn(low, cc))
            join = lambda parts: jnp.concatenate([parts[1][:HALF_T] + parts[0], parts[1][HALF_T:]], axis=0)
            halves.append(
                (jnp.concatenate(outs, axis=0), jnp.concatenate(grads_q, axis=0), join(grads_k), join(grads_v))
            )
        first = (lax.broadcasted_iota(jnp.int32, (1, 128), 1) // HD) == 0
        result, dq, dk, dv = (jnp.where(first, a, b) for a, b in zip(*halves))
        ctx[:, cols] = result.astype(BF16)
        for n, field in enumerate((dq, dk, dv)):
            if n < 2:
                field = rotated(field, cos_t[...], left_t[...], right_t[...], -1.0)
            field = field.astype(BF16)
            tb[:, span(n * 384 + pair * 128, 128)] = field
            gvec[0:1, span(5 * D + n * 384 + pair * 128, 128)] = jnp.sum(field.astype(F32), axis=0, keepdims=True)

        @pl.when(pair == 0)
        def _():
            gather.finish(1)
            gather.turn(2)

        @pl.when(pair == 1)
        def _():
            gather.forward(2)

        return carry

    lax.fori_loop(0, 3, attend, 0)
    gather.finish(2)

    for i in range(2):
        rows = slice(384 * i, 384 * i + 384)
        put(i, 0, nn(s1t[rows, :], tb[...]))
        put(i, G_DENSE, nn(upt[rows, :], ctx[...]))
    for part in range(2):
        reduce.pull(0, part)
    for i in range(2):
        rows = slice(384 * i, 384 * i + 384)
        outp[:, rows] = nt(ctx[...], wrows(i, W_DENSE, 384))
        first = nt(tb[...], wrows(i, 0, 1152))
        nbp[:, rows] = first * vec[0:1, rows]
        gvec[0:1, rows] = jnp.sum(first * hat[:, rows], axis=0, keepdims=True)
        gvec[0:1, slice(2 * D + 384 * i, 2 * D + 384 * i + 384)] = jnp.sum(first, axis=0, keepdims=True)
    gather.done(1)
    reduce.start(0)

    for half in range(2):
        base = W_UNITS[half]
        lane = 5 * D + 1152 + half * 768

        def units(i, carry, base=base, lane=lane):
            cols = span(i * 256, 256)
            pre = nn(s2[...], wcols(base + i * 256, 256)) + rowvec(lane + i * 256, 256)
            phi = 0.5 * (1.0 + lax.erf(pre * (1.0 / math.sqrt(2.0))))
            act[:, cols] = (pre * phi).astype(BF16)
            slope = phi + pre * jnp.exp(-0.5 * pre * pre) * (1.0 / math.sqrt(2.0 * math.pi))
            back = (nn(up[...], wcols(base + 768 + i * 256, 256)) * slope).astype(BF16)
            ub[:, cols] = back
            gvec[0:1, span(lane + i * 256, 256)] = jnp.sum(back.astype(F32), axis=0, keepdims=True)
            return carry

        lax.fori_loop(0, 3, units, 0)
        if half == 0:
            reduce.turn(0)
        else:
            reduce.done(0, pick_t, quad_out)
            reduce.turn(1)
        for i in range(2):
            rows = slice(384 * i, 384 * i + 384)
            put(i, G_INNER[half], nn(s2t[rows, :], ub[...]))
            put(i, G_OUTER[half], nn(upt[rows, :], act[...]))
        if half == 0:
            for part in range(2):
                reduce.pull(1, part)
        else:
            reduce.pull(2, 0)
        for i in range(2):
            rows = slice(384 * i, 384 * i + 384)
            outp[:, rows] += nt(act[...], wrows(i, base + 768, 768))
            second = nt(ub[...], wrows(i, base, 768))
            if half == 0:
                sec[:, rows] = second
            else:
                second += sec[:, rows]
                nbp[:, rows] += second * vec[0:1, D + 384 * i : D + 384 * i + 384]
                gvec[0:1, D + 384 * i : D + 384 * i + 384] = jnp.sum(second * hat[:, rows], axis=0, keepdims=True)
                gvec[0:1, 3 * D + 384 * i : 3 * D + 384 * i + 384] = jnp.sum(second, axis=0, keepdims=True)
        if half == 0:
            gather.done(2)
            reduce.finish(0)
            reduce.start(1)

    tile = jnp.zeros((64, 128), F32)
    for begin in range(0, VEC, D):
        width = min(D, VEC - begin)
        cols = slice(begin, begin + width)
        tile += nt((gvec[0:1, cols] * mask[:, cols].astype(F32)).astype(BF16), spread[:, cols])
    tile = nn(rows_at[...], tile.astype(BF16)).astype(BF16)
    g[:, :, :, G_SMALL : G_SMALL + 128] = tile.reshape(Y, Z, BLK, 128)
    g[:, :, :, COLS - 128 : COLS] = jnp.zeros((Y, Z, BLK, 128), BF16)
    reduce.pull(2, 1)
    reduce.start(2)

    own = me.t * HALF_T
    other = pl.ds(pl.multiple_of((1 - me.t) * HALF_T, HALF_T), HALF_T)
    out_send[...] = outp[other, :].astype(BF16)
    nb_send[...] = nbp[other, :].astype(BF16)
    for i, (src, dst) in enumerate(((out_send, out_land), (nb_send, nb_land))):
        swaps.append(Copy(lambda src=src, dst=dst, i=i: (src, dst, ts.at[2 + i], tr.at[2 + i], partner)))
    reduce.finish(1)
    reduce.turn(2)
    for copy in swaps[2:]:
        copy.wait_recv()

    def finish_rows(i, carry):
        rows = pl.ds(pl.multiple_of(i * 64, 64), 64)
        mine_at = pl.ds(pl.multiple_of(own + i * 64, 64), 64)
        low = (nn(x[rows, :], perm[...]) + outp[mine_at, :] + out_land[rows, :].astype(F32) + fb).astype(BF16)
        out[rows, :] = nt(low, perm[...]).astype(BF16)
        back = nbp[mine_at, :] + nb_land[rows, :].astype(F32)
        normal = hat[mine_at, :]
        value = up[mine_at, :].astype(F32) + fac[mine_at, 0:1] * (
            back
            - jnp.mean(back, axis=-1, keepdims=True)
            - normal * jnp.mean(back * normal, axis=-1, keepdims=True)
        )
        grad[rows, :] = nt(value.astype(BF16), perm[...]).astype(BF16)
        return carry

    lax.fori_loop(0, 4, finish_rows, 0)
    reduce.done(1, pick_t, quad_out)
    reduce.finish(2)
    reduce.done(2, pick_t, quad_out)
    owners = []
    for r in (1, 2, 3):

        def parts(r=r):
            device, xh, c = me.quad(r)
            return quad_out.at[xh * 2 + c], quad_land.at[me.slot], qs.at[1, r], qr.at[1, r], device

        owners.append(Copy(parts))
    quad_land[me.slot] = quad_out[me.slot]
    for copy in owners:
        copy.wait_recv()
    small_mine[...] = quad_land[0, :, WIDE - 128 :].astype(F32) + quad_land[2, :, WIDE - 128 :].astype(F32)
    last = Copy(lambda: (small_mine, small_land, es, er, partner))
    for c in range(2):
        rows_out[c] = quad_land[c].astype(F32) + quad_land[2 + c].astype(F32)
    for copy in quads + swaps + owners:
        copy.wait_send()
    gather.sent()
    reduce.sent()
    last.wait_send()
    last.wait_recv()
    lane = lax.broadcasted_iota(jnp.int32, (PAD, 128), 1)
    small_out[...] = small_mine[...] + jnp.where(lane < 4 * OWN, small_land[...], 0.0)


def turn_tables(starts):
    places = (jnp.arange(T, dtype=jnp.int32) - starts).astype(F32)
    lane = jnp.arange(128, dtype=jnp.int32) % HD
    freqs = jnp.exp((lane % 8).astype(F32) * (-2.0 * math.log(10000.0) / ROT))
    turns = places[:, None] * freqs[None, :]
    cosine, sine = jnp.cos(turns), jnp.sin(turns)
    return (
        jnp.where(lane < ROT, cosine, 1.0),
        jnp.where(lane < 8, -sine, 0.0),
        jnp.where((lane >= 8) & (lane < ROT), sine, 0.0),
    )


def local(
    layer_input, segment_starts, norm_gains, norm_shifts, projection, triple_bias, dense_weight, inner_weight,
    unit_bias, outer_weight, final_bias, cotangent,
):
    small = jnp.concatenate(
        [norm_gains.reshape(-1), norm_shifts.reshape(-1), final_bias, triple_bias.reshape(-1), unit_bias]
    )
    small = jnp.pad(small[None, :], ((0, OWN - 1), (0, 128 - small.shape[0])))
    triple = projection.reshape(OWN, 1152)
    mine = jnp.concatenate(
        [triple[:, :896], inner_weight, triple[:, 896:], small, dense_weight.T, jnp.zeros((OWN, 128), BF16), outer_weight.T],
        axis=1,
    )
    mine = jnp.pad(mine, ((0, PAD - OWN), (0, 0)))
    mine = jnp.stack([mine[:, :WIDE], mine[:, WIDE:]])
    start_col = jnp.broadcast_to(segment_starts[:, None], (T, 128))
    start_row = jnp.broadcast_to(segment_starts[None, :], (8, T))
    vm = pl.BlockSpec(memory_space=pltpu.VMEM)
    dma = pltpu.SemaphoreType.DMA
    struct = jax.ShapeDtypeStruct
    vmem = pltpu.VMEM
    out, grad, small_grad, rows_grad = pl.pallas_call(
        kernel,
        out_shape=(
            struct((HALF_T, D), BF16), struct((HALF_T, D), BF16), struct((PAD, 128), F32), struct((2, PAD, WIDE), F32),
        ),
        in_specs=[vm] * 15,
        out_specs=(vm,) * 4,
        scratch_shapes=[
            vmem((Y, Z, BLK, COLS), BF16), vmem((Y, Z, BLK, COLS), BF16), vmem((Y, Z, BLK, WIDE), BF16),
            vmem((4, BLK, WIDE), BF16), vmem((2, 4, BLK, WIDE), BF16), vmem((3, BLK, WIDE), BF16),
            vmem((4, PAD, WIDE), BF16), vmem((4, PAD, WIDE), BF16), vmem((4, PAD, WIDE), BF16),
        ]
        + [vmem((HALF_T, D), BF16)] * 6
        + [vmem((PAD, 128), F32)] * 2
        + [vmem((T, D), BF16)] * 3
        + [vmem((D, T), BF16)] * 3
        + [vmem((T, D), F32), vmem((T, 128), F32)]
        + [vmem((T, 384), BF16)] * 5
        + [vmem((T, 1152), BF16), vmem((T, 768), BF16), vmem((T, 768), BF16)]
        + [vmem((T, D), F32)] * 3
        + [vmem((8, VEC), F32)] * 2
        + [dma((3, 2, 3))] * 2
        + [dma((3, 2, 4))] * 4
        + [dma((3, 2, 4))] * 4
        + [dma((3, 2, 3))] * 2
        + [dma((2, 4))] * 2
        + [dma((4,))] * 2
        + [dma] * 2,
        compiler_params=pltpu.CompilerParams(collective_id=0, has_side_effects=True, vmem_limit_bytes=VMEM_LIMIT),
        name="layer",
    )(
        mine, layer_input, cotangent, *[jnp.asarray(m) for m in order_tables()], *turn_tables(segment_starts),
        start_col, start_row,
    )

    vals = small_grad[0]
    side = lax.axis_index("tensor")

    def six(field):
        return lax.dynamic_slice_in_dim(field, side * 6, 6, axis=field.ndim - 1)

    a, b = rows_grad[0, :OWN], rows_grad[1, :OWN]
    return (
        out,
        grad,
        six(vals[0:24].reshape(2, OWN)),
        six(vals[24:48].reshape(2, OWN)),
        jnp.concatenate([a[:, :768], b[:, :384]], axis=1).reshape(OWN, 3, 384),
        vals[OFF_TB:OFF_UB].reshape(3, 6),
        b[:, 384:768].T,
        a[:, 768:2304],
        vals[OFF_UB : OFF_UB + 24],
        b[:, 768:2304].T,
        six(vals[48:60]),
    )


def solution(mesh):
    placed = (
        P(("dp", "tensor"), None),
        P("dp"),
        P(None, "dp"),
        P(None, "dp"),
        P("dp", None, "tensor"),
        P(None, ("tensor", "dp")),
        P("tensor", "dp"),
        P("dp", "tensor"),
        P(("tensor", "dp")),
        P("tensor", "dp"),
        P("dp"),
        P(("dp", "tensor"), None),
    )
    return jax.shard_map(
        local,
        mesh=mesh,
        in_specs=placed,
        out_specs=(
            P(("dp", "tensor"), None),
            P(("dp", "tensor"), None),
            P(None, ("dp", "tensor")),
            P(None, ("dp", "tensor")),
            P("dp", None, "tensor"),
            P(None, ("tensor", "dp")),
            P("tensor", "dp"),
            P("dp", "tensor"),
            P(("tensor", "dp")),
            P("tensor", "dp"),
            P(("dp", "tensor")),
        ),
        check_vma=False,
    )
```

time: 161 us -> 144 us (0.89)
  Pallas kernels: 133 us -> 120 us
  local copies, waits for them, and re-layouts: 23.9 us -> 19 us
    pallas_call x3 -> x1, Pallas kernels: 133 us -> 120 us  [local(): pl.pallas_call(kernel, out_shape=(struct((HALF_T, D), BF16), struct((HALF...]
    unnamed x9 -> x16, local copies, waits for them, and re-layouts: 6.66 us -> 3.85 us
    transpose x2, local copies, waits for them, and re-layouts: 2.97 us -> 1.26 us  [the longest x1 0.65 us: local(): b[:, 768:2304]]
where the time goes in v2:
time: 144 us; the launch traced here: 143 us
  Pallas kernels  120 us (83%)
  local copies, waits for them, and re-layouts  19 us (13%)
  other arithmetic  3.28 us (2%)
    pallas_call x1, Pallas kernels, local(): pl.pallas_call(kernel, out_shape=(struct((HALF_T, D), BF16), struct((HALF...  120 us
    unnamed x16, local copies, waits for them, and re-layouts  3.85 us

profile of v2, /device:TPU:1, one launch (start us, length us, event | category | flops | bytes accessed | tf_op | source)
XLA Modules:
  0.0 143.3 jit_solution(14892968416459225109)
XLA Ops:
  0.7 0.8 pad.14
  1.5 0.8 constant_dynamic-update-slice_fusion.4
  2.3 0.7 reshape.82
  3.0 0.7 reshape.83
  3.8 0.8 reshape.84
  4.5 1.4 concatenate.9
  6.0 0.7 constant_dynamic-update-slice_fusion.1
  6.7 0.8 bitcast_dynamic-update-slice_fusion
  7.5 0.7 pad_maximum_fusion.mine
  8.2 0.7 subtract_convert_fusion
  8.9 1.9 %fusion = (f32[512,128]{1,0:T(8,128)}, f32[512,128]{1,0:T(8,128)}, f32[512,128]{1,0:T(8,128)}) fusion(f32[128]{0:T(128)S(1)} %fusion.9, f32[512]{0:T(512)S(1)} %subtract_convert_fusion, pred[128]{0:T(512)(128)(4,1)S(1)} %get-tuple-element.31, pred[128]{0:T(512)(128)(4,1)S(1)} %get-tuple-element.32, pred[128]{0:T(512)(128)(4,1)S(1)} %broadcast_compare_fusion.1), kind=kLoop, calls=%fused_computation.2 | loop fusion | flops 327680 | bytes 789376 | tf_op jit(solution)/shard_map/jit(_where)/select_n | solution.py:662
  10.8 0.9 broadcast_in_dim.45.start_col
  12.3 120.3 %layer.1 = (bf16[256,768]{1,0:T(8,128)(2,1)}, bf16[256,768]{1,0:T(8,128)(2,1)}, f32[16,128]{1,0:T(8,128)}, f32[2,16,2432]{2,1,0:T(8,128)}) custom-call(bf16[2,16,2432]{2,1,0:T(8,128)(2,1)} %pad_maximum_fusion.mine, bf16[256,768]{1,0:T(8,128)(2,1)} %x.5, bf16[256,768]{1,0:T(8,128)(2,1)} %cot.1, bf16[768,768]{1,0:T(8,128)(2,1)} %constant.66.clone.perm, ...), custom_call_target="tpu_custom_call" | custom-call | tf_op jit(solution)/shard_map/layer/pallas_call | solution.py:687
  132.6 1.1 slice_bitcast_fusion.1
  134.3 0.7 reshape.87
  134.9 1.4 slice_reduce_fusion.1
  136.4 0.6 constant_dynamic-slice_fusion.1
  137.7 0.8 slice.77
  139.1 0.6 slice.83
  139.7 0.6 slice_bitcast_fusion.2
  140.4 0.8 slice_reduce_fusion
  141.1 0.7 reshape.88
  141.8 0.7 copy.39
  142.6 0.7 copy.40
  (23 shorter events, 2.7 us)
Async XLA Ops:
  0.6 10.2 %copy-start.2 = (s32[512]{0:T(512)S(1)}, s32[512]{0:T(512)}, u32[]{:S(2)}) copy-start(s32[512]{0:T(512)} %param.20) | copy-start | bytes 6148
  132.5 9.3 %copy-start.1 = (bf16[256,768]{1,0:T(8,128)(2,1)S(1)}, bf16[256,768]{1,0:T(8,128)(2,1)}, u32[]{:S(2)}) copy-start(bf16[256,768]{1,0:T(8,128)(2,1)} %get-tuple-element.44) | copy-start | bytes 1179652
  132.5 10.0 %copy-start = (bf16[256,768]{1,0:T(8,128)(2,1)S(1)}, bf16[256,768]{1,0:T(8,128)(2,1)}, u32[]{:S(2)}) copy-start(bf16[256,768]{1,0:T(8,128)(2,1)} %get-tuple-element.45) | copy-start | bytes 1179652

commit v3 on v2

--- a/solution.py
+++ b/solution.py
@@ -20,11 +20,12 @@
 BLK = OWN * XH * CORE
 COLS, WIDE = 4864, 2432
 W_SMALL, W_DENSE, W_UNITS = 1152, 1280, (1792, 3328)
-G_DENSE, G_INNER, G_OUTER, G_SMALL = 1152, (1536, 3072), (2304, 3968), 3840
+G_COLS, G_WIDE = 4608, 2304
+G_DENSE, G_INNER, G_OUTER = 1152, (1536, 3072), (2304, 3840)
 EVEN = ((0, 384), (384, 384))
 UNEVEN = ((0, 512), (512, 384))
 W_GROUPS = ((0, 896, UNEVEN, 0), (1792, 768, EVEN, 896), (3328, 768, EVEN, 1664))
-G_GROUPS = ((0, 768, EVEN, 0), (1536, 768, EVEN, 768), (3072, 896, UNEVEN, 1536))
+G_GROUPS = ((0, 768, EVEN, 0), (1536, 768, EVEN, 768), (3072, 768, EVEN, 1536))
 VEC = 5 * D + 3 * 384 + 1536
 OFF_TB, OFF_UB = 5 * OWN, 5 * OWN + 18
 VMEM_LIMIT = 56 * 1024 * 1024
@@ -53,10 +54,12 @@
     mask[back[col // 24], 5 * D + 1152 + col] = 1
     rows = np.zeros((D, 64), np.float32)
     rows[12 * j, j] = 1
+    eights = np.zeros((128, 64), np.float32)
+    eights[8 * (j // 4) + j % 4, j] = 1
     pick = np.zeros((BLK, 64), np.float32)
     r = np.arange(BLK)
     pick[r, 16 * (r // 12) + r % 12] = 1
-    return [m.astype(jnp.bfloat16) for m in (perm, spread, mask, rows, np.ascontiguousarray(rows.T), pick, np.ascontiguousarray(pick.T))]
+    return [m.astype(jnp.bfloat16) for m in (perm, spread, mask, eights, np.ascontiguousarray(rows.T), pick, np.ascontiguousarray(pick.T))]
 
 
 def nn(a, b):
@@ -98,11 +101,16 @@
         xh = 1 - self.xh if r & 2 else self.xh
         return self.dev(xh=xh, c=c), xh, c
 
+    def other(self, r):
+        c = 1 - self.c if r & 1 else self.c
+        xh = 1 - self.xh if r & 2 else self.xh
+        return self.dev(xh=xh, c=c, t=1 - self.t)
+
     def peers(self):
         out = [self.quad(r)[0] for r in (1, 2, 3)]
         for axis in ("y", "z"):
             out += [self.ring(axis, step) for step in (1, 2, 3)]
-        return out + [self.dev(t=1 - self.t)]
+        return out + [self.other(r) for r in range(4)]
 
 
 def enter(place):
@@ -194,7 +202,9 @@
             for step in (1, 3, 2):
                 self.first[group, part, step - 1].wait_recv()
             for i, step in enumerate((1, 3)):
-                self.onward(group, part, 0, None, i, step)
+                self.onward(group, part, 0, i, i, step)
+            for i, step in enumerate((1, 3)):
+                self.onward(group, part, 0, 1 - i, 4 + i, step)
             self.share(group, part, 0)
 
     def forward(self, group):
@@ -202,9 +212,12 @@
             for i, step in enumerate((1, 3)):
                 self.second[group, part, i].wait_recv()
                 self.onward(group, part, 4 - step, i, 2 + i, step)
+
+    def finish(self, group):
+        for part in range(2):
+            for i, step in enumerate((1, 3)):
+                self.second[group, part, 4 + i].wait_recv()
                 self.share(group, part, 4 - step)
-
-    def finish(self, group):
         for part in range(2):
             for i in range(2):
                 self.second[group, part, 2 + i].wait_recv()
@@ -228,7 +241,7 @@
         self.me, self.g, self.land, self.ring1, self.ring2, self.red = me, g, land, ring1, ring2, red
         self.cs, self.cr, self.p0s, self.p0r, self.p1s, self.p1r = sems
         self.sibling = me.dev(c=1 - me.c)
-        self.pulled, self.first, self.second = {}, {}, {}
+        self.pulled, self.first, self.second, self.delivered = {}, {}, {}, {}
 
     def place(self, group, part, piece=None):
         _, _, parts, at = G_GROUPS[group]
@@ -292,24 +305,29 @@
                     return src, dst, self.p0s.at[at], self.p0r.at[at], self.me.ring(self.axes[part][0], step)
 
                 self.first[group, part, i] = Copy(parts)
-
-    def whole2(self, group, part, i):
-        _, at, width = self.place(group, part)
-        return self.ring2.at[i, :, :, span(at, width)]
-
-    def turn(self, group):
         for part in range(2):
             for i, step in enumerate((1, 3)):
                 self.join(group, part, step)
+                self.owner(group, part, i, 1 - i, 4 + i, step)
+
+    def owner(self, group, part, i, piece, sem, step):
+        def parts():
+            at = (group, part, sem)
+            src, dst = self.unit(group, part, step, piece), self.whole2(group, part, i, piece)
+            return src, dst, self.p0s.at[at], self.p0r.at[at], self.me.ring(self.axes[part][0], step)
+
+        self.first[group, part, sem] = Copy(parts)
+
+    def whole2(self, group, part, i, piece=None):
+        _, at, width = self.place(group, part, piece)
+        return self.ring2.at[i, :, :, span(at, width)]
+
+    def turn(self, group):
+        for part in range(2):
+            for i, step in enumerate((1, 3)):
                 self.first[group, part, i].wait_recv()
                 self.add(self.unit(group, part, step, i), self.piece1(group, part, i))
-
-                def parts(part=part, i=i, step=step):
-                    at = (group, part, 2 + i)
-                    src, dst = self.unit(group, part, step), self.whole2(group, part, i)
-                    return src, dst, self.p0s.at[at], self.p0r.at[at], self.me.ring(self.axes[part][0], step)
-
-                self.first[group, part, 2 + i] = Copy(parts)
+                self.owner(group, part, i, i, 2 + i, step)
 
     def across(self, group, part, step):
         me = self.me
@@ -324,6 +342,7 @@
         for part in range(2):
             self.join(group, part, 0)
             for i in range(2):
+                self.first[group, part, 4 + i].wait_recv()
                 self.first[group, part, 2 + i].wait_recv()
             self.add(self.unit(group, part, 0), self.whole2(group, part, 0), self.whole2(group, part, 1))
             for step in (2, 1, 3):
@@ -345,10 +364,85 @@
                 total += self.red[step - 1, :, at : at + width].astype(F32)
             quad[:, :, at : at + width] = nn(pick_t[...], total.astype(BF16)).astype(BF16).reshape(4, PAD, width)
 
+    def deliver(self, group, quad, landing, qs, qr):
+        me = self.me
+        _, half, _, at = G_GROUPS[group]
+        for r in (1, 2, 3):
+
+            def parts(r=r):
+                device, xh, c = me.quad(r)
+                src, dst = quad.at[xh * 2 + c, :, span(at, half)], landing.at[me.slot, :, span(at, half)]
+                return src, dst, qs.at[1, group, r], qr.at[1, group, r], device
+
+            self.delivered[group, r] = Copy(parts)
+        landing[me.slot, :, at : at + half] = quad[me.slot, :, at : at + half]
+
     def sent(self):
-        for copies in (self.pulled, self.first, self.second):
+        for copies in (self.pulled, self.first, self.second, self.delivered):
             for copy in copies.values():
                 copy.wait_send()
+
+
+class Small:
+    def __init__(self, me, mine, land_z, land_y, land_q, sends, recvs):
+        self.me, self.mine, self.land_z, self.land_y, self.land_q = me, mine, land_z, land_y, land_q
+        self.sends, self.recvs, self.copies = sends, recvs, {}
+
+    def copy(self, n, src, dst, device):
+        self.copies[n] = Copy(lambda: (src(), dst(), self.sends.at[n], self.recvs.at[n], device()))
+
+    def start(self):
+        me = self.me
+        for step in (2, 1, 3):
+            self.copy(
+                step - 1,
+                lambda step=step: self.mine.at[:, lax.rem(me.z + step, 4)],
+                lambda step=step: self.land_z.at[step - 1],
+                lambda step=step: me.ring("z", step),
+            )
+
+    def turn(self):
+        me = self.me
+        for n in range(3):
+            self.copies[n].wait_recv()
+        self.land_z[3] = self.mine[:, me.z] + self.land_z[0] + self.land_z[1] + self.land_z[2]
+        for step in (2, 1, 3):
+            self.copy(
+                2 + step,
+                lambda step=step: self.land_z.at[3, lax.rem(me.y + step, 4)],
+                lambda step=step: self.land_y.at[step - 1],
+                lambda step=step: me.ring("y", step),
+            )
+
+    def finish(self):
+        me = self.me
+        for n in range(3):
+            self.copies[3 + n].wait_recv()
+        self.land_y[3] = self.land_z[3, me.y] + self.land_y[0] + self.land_y[1] + self.land_y[2]
+        place = me.t * 4 + me.slot
+        self.land_q[place] = self.land_y[3]
+        for r in range(7):
+            self.copy(
+                6 + r,
+                lambda: self.land_y.at[3],
+                lambda: self.land_q.at[me.t * 4 + me.slot],
+                lambda r=r: me.quad(r + 1)[0] if r < 3 else me.other(r - 3),
+            )
+
+    def done(self):
+        me = self.me
+        for r in range(7):
+            self.copies[6 + r].wait_recv()
+        lane = lax.broadcasted_iota(jnp.int32, (8, 128), 1)
+        row = lax.broadcasted_iota(jnp.int32, (8, 128), 0)
+        total = jnp.zeros((8, 128), F32)
+        for n in range(4):
+            total += self.land_q[me.t * 4 + n] + jnp.where(lane < 4 * OWN, self.land_q[(1 - me.t) * 4 + n], 0.0)
+        return jnp.broadcast_to(jnp.sum(jnp.where(row == me.slot, total, 0.0), axis=0, keepdims=True), (8, 128))
+
+    def sent(self):
+        for copy in self.copies.values():
+            copy.wait_send()
 
 
 def rotated(field, cosine, left, right, sign):
@@ -356,39 +450,136 @@
     return field * cosine + sign * (pltpu.roll(field, n - 8, 1) * left + pltpu.roll(field, 8, 1) * right)
 
 
+def one_hot(shape, test):
+    row = lax.broadcasted_iota(jnp.int32, shape, 0)
+    col = lax.broadcasted_iota(jnp.int32, shape, 1)
+    return jnp.where(test(row, col), 1.0, 0.0)
+
+
+def pack(triple, dense, inner, outer, small, mine):
+    mine[...] = jnp.zeros_like(mine)
+    tall = one_hot((PAD, OWN), lambda r, c: r == c).astype(BF16)
+    line = jnp.zeros((1, 128), F32)
+    begin = 0
+    for ref in small:
+        count, width = ref.shape
+        for i in range(count):
+            put = one_hot((width, 128), lambda r, c, begin=begin: c == r + begin).astype(BF16)
+            line += nn(ref[i : i + 1, :], put)
+            begin += width
+    first = lax.broadcasted_iota(jnp.int32, (PAD, 128), 0) == 0
+    rows = nn(tall, triple[...]).astype(BF16)
+    mine[0, :, 0:896] = rows[:, 0:896]
+    mine[0, :, 896:WIDE] = nn(tall, inner[...]).astype(BF16)
+    mine[1, :, 0:256] = rows[:, 896:1152]
+    mine[1, :, 256:384] = jnp.where(first, line, 0.0).astype(BF16)
+    mine[1, :, 384:768] = nn(tall, dense[...]).astype(BF16)
+    mine[1, :, 896:WIDE] = nn(tall, outer[...]).astype(BF16)
+
+
+def turn_tables(starts, cos_t, left_t, right_t, bias):
+    begin = jnp.broadcast_to(starts[...].astype(F32), (8, T))
+    places = lax.broadcasted_iota(jnp.int32, (8, T), 1).astype(F32) - begin
+    freqs = jnp.exp(lax.broadcasted_iota(jnp.int32, (8, T), 0).astype(F32) * (-2.0 * math.log(10000.0) / ROT))
+    turns = places * freqs
+
+    def spread_lanes(rows, test):
+        put = one_hot((8, 128), lambda r, c: (c % 8 == r) & test(c % HD))
+        return lax.dot_general(
+            rows.T, put, (((1,), (0,)), ((), ())), preferred_element_type=F32, precision=lax.Precision.HIGHEST
+        )
+
+    lane = lax.broadcasted_iota(jnp.int32, (1, 128), 1) % HD
+    sine = jnp.sin(turns)
+    cos_t[...] = spread_lanes(jnp.cos(turns), lambda c: c < ROT) + jnp.where(lane < ROT, 0.0, 1.0)
+    left_t[...] = -spread_lanes(sine, lambda c: c < ROT // 2)
+    right_t[...] = spread_lanes(sine, lambda c: (c >= ROT // 2) & (c < ROT))
+    begin_col = begin.T[:, 0:1]
+
+    def body(i, carry):
+        rows = pl.ds(pl.multiple_of(i * 128, 128), 128)
+        place_t = i * 128 + lax.broadcasted_iota(jnp.int32, (128, T), 0)
+        place_s = lax.broadcasted_iota(jnp.int32, (128, T), 1)
+        col = bias[rows, 0:1]
+        bias[rows, :] = jnp.where((col == begin[0:1, :]) & (place_s <= place_t), 0.0, -1e30)
+        return carry
+
+    bias[:, 0:128] = jnp.broadcast_to(begin_col, (T, 128))
+    lax.fori_loop(0, 4, body, 0)
+
+
+def unpack_kernel(rows, small, gains, shifts, triple_b, units, final, proj, dense, inner, outer):
+    side = lax.axis_index("tensor")
+    line = jnp.broadcast_to(small[0:1, :], (8, 128))
+
+    def lanes(begin, width):
+        put = one_hot((128, width), lambda r, c: r == c + begin)
+        picked = lax.dot_general(
+            line, put, (((1,), (0,)), ((), ())), preferred_element_type=F32, precision=lax.Precision.HIGHEST
+        )
+        return picked[0:1, :]
+
+    for i in range(2):
+        gains[i : i + 1, :] = lanes(OWN * i + side * 6, 6)
+        shifts[i : i + 1, :] = lanes(2 * OWN + OWN * i + side * 6, 6)
+    for i in range(3):
+        triple_b[i : i + 1, :] = lanes(OFF_TB + 6 * i, 6)
+    units[...] = lanes(OFF_UB, 24)
+    final[...] = lanes(4 * OWN + side * 6, 6)
+    proj[:, 0:768] = rows[0, 0:OWN, 0:768]
+    proj[:, 768:1152] = rows[1, 0:OWN, 0:384]
+    inner[...] = rows[0, 0:OWN, 768:2304]
+    dense[...] = rows[1, 0:OWN, 384:768]
+    outer[...] = rows[1, 0:OWN, 768:2304]
+
+
 def kernel(
-    mine, x, cot, perm, spread, mask, rows_at, rows_of, pick, pick_t, cos_t, left_t, right_t, start_col, start_row,
+    triple, dense, inner_w, outer_w, gains, shifts, fbias, tbias, ubias, starts, x, cot,
+    perm, spread, mask, rows_at, rows_of, pick, pick_t,
     out, grad, small_out, rows_out,
     w, g, land, ring1, ring2, red, quad_in, quad_out, quad_land, x_land, cot_land, out_send, out_land, nb_send, nb_land,
-    small_mine, small_land,
-    s1, s2, up, s1t, s2t, upt, hat, fac, q, k, v, cb, ctx, tb, act, ub, outp, sec, nbp, vec, gvec,
+    small_mine, small_z, small_y, small_q,
+    s1, s2, up, s1t, s2t, upt, hat, fac, q, k, v, cb, ctx, tb, act, ub, outp, nbp, vec, gvec,
+    mine, cos_t, left_t, right_t, bias, slope,
     ap0s, ap0r, ap1s, ap1r, ass, asr, rcs, rcr, rp0s, rp0r, rp1s, rp1r, qs, qr, ts, tr, es, er,
 ):
     me = Place()
+    pack(triple, dense, inner_w, outer_w, (gains, shifts, fbias, tbias, ubias), mine)
     enter(me)
     partner = me.dev(t=1 - me.t)
     gather = Gather(me, w, (ap0s, ap0r, ap1s, ap1r, ass, asr))
     reduce = Reduce(me, g, land, ring1, ring2, red, (rcs, rcr, rp0s, rp0r, rp1s, rp1r))
-    quads, swaps = [], []
-    for r in (1, 2, 3):
-
-        def parts(r=r):
-            device, _, c = me.quad(r)
-            return mine.at[c], quad_in.at[me.slot], qs.at[0, r], qr.at[0, r], device
-
-        quads.append(Copy(parts))
-    for i, (src, dst) in enumerate(((x, x_land), (cot, cot_land))):
-        swaps.append(Copy(lambda src=src, dst=dst, i=i: (src, dst, ts.at[i], tr.at[i], partner)))
+    minor = Small(me, small_mine, small_z, small_y, small_q, es, er)
+    quads, swaps = {}, []
+    for group, (_, half, _, at) in enumerate(W_GROUPS):
+        for r in (1, 2, 3):
+
+            def parts(group=group, half=half, at=at, r=r):
+                device, _, c = me.quad(r)
+                src, dst = mine.at[c, :, span(at, half)], quad_in.at[me.slot, :, span(at, half)]
+                return src, dst, qs.at[0, group, r], qr.at[0, group, r], device
+
+            quads[group, r] = Copy(parts)
+
+    def swap(i, src, dst):
+        swaps.append(Copy(lambda: (src, dst, ts.at[i], tr.at[i], partner)))
+
     quad_in[me.slot] = mine[me.c]
     gvec[...] = jnp.zeros_like(gvec)
-    for copy in quads:
-        copy.wait_recv()
-    block = nn(pick[...], quad_in[...].reshape(64, WIDE)).astype(BF16)
-    for base, half, _, at in W_GROUPS:
-        w[me.y, me.z, :, span(me.c * half + base, half)] = block[:, at : at + half]
-    gather.start(0)
-
-    def norm_rows(x_ref, cot_ref, first_row):
+    turn_tables(starts, cos_t, left_t, right_t, bias)
+    swap(0, x, x_land)
+
+    def block(group):
+        base, half, _, at = W_GROUPS[group]
+        for r in (1, 2, 3):
+            quads[group, r].wait_recv()
+        rows = quad_in[:, :, at : at + half].reshape(64, half)
+        w[me.y, me.z, :, span(me.c * half + base, half)] = nn(pick[...], rows).astype(BF16)
+        gather.start(group)
+
+    block(0)
+    swap(1, cot, cot_land)
+    def norm_rows(x_ref, first_row):
         def body(i, carry):
             src = pl.ds(pl.multiple_of(i * 128, 128), 128)
             rows = pl.ds(pl.multiple_of(first_row + i * 128, 128), 128)
@@ -398,6 +589,14 @@
             factor = lax.rsqrt(jnp.mean(centred * centred, axis=-1, keepdims=True) + EPSILON)
             hat[rows, :] = centred * factor
             fac[rows, :] = jnp.broadcast_to(factor, (128, 128))
+            return carry
+
+        lax.fori_loop(0, 2, body, 0)
+
+    def back_rows(cot_ref, first_row):
+        def body(i, carry):
+            src = pl.ds(pl.multiple_of(i * 128, 128), 128)
+            rows = pl.ds(pl.multiple_of(first_row + i * 128, 128), 128)
             upstream = nn(cot_ref[src, :], perm[...])
             up[rows, :] = upstream.astype(BF16)
             upt[:, rows] = upstream.astype(BF16).T
@@ -406,16 +605,16 @@
 
         lax.fori_loop(0, 2, body, 0)
 
-    norm_rows(x, cot, me.t * HALF_T)
+    norm_rows(x, me.t * HALF_T)
     gather.turn(0)
-    gather.start(1)
-    for copy in swaps:
-        copy.wait_recv()
-    norm_rows(x_land, cot_land, (1 - me.t) * HALF_T)
+    back_rows(cot, me.t * HALF_T)
+    block(1)
     gather.forward(0)
+    swaps[0].wait_recv()
+    norm_rows(x_land, (1 - me.t) * HALF_T)
     gather.finish(0)
     gather.turn(1)
-    gather.start(2)
+    block(2)
     gather.done(0)
 
     def wcols(begin, width):
@@ -452,6 +651,10 @@
         return carry
 
     lax.fori_loop(0, 4, scale_rows, 0)
+    swaps[1].wait_recv()
+    back_rows(cot_land, (1 - me.t) * HALF_T)
+
+    scale = 1.0 / math.sqrt(HD)
 
     def heads_in(i, carry):
         cols = span(i * 128, 128)
@@ -459,14 +662,13 @@
             field = nn(s1[...], wcols(n * 384 + i * 128, 128)) + rowvec(5 * D + n * 384 + i * 128, 128)
             if n < 2:
                 field = rotated(field, cos_t[...], left_t[...], right_t[...], 1.0)
-            ref[:, cols] = field.astype(BF16)
+            field = field.astype(BF16)
+            ref[:, cols] = field * BF16(scale) if n == 0 else field
         cb[:, cols] = nn(up[...], wcols(W_DENSE + i * 128, 128)).astype(BF16)
         return carry
 
     lax.fori_loop(0, 3, heads_in, 0)
     gather.forward(1)
-
-    scale = 1.0 / math.sqrt(HD)
 
     def attend(pair, carry):
         cols = span(pair * 128, 128)
@@ -480,19 +682,16 @@
                 kk, vv = k[0:n, cols], v[0:n, cols]
                 qq = jnp.where(inside, q[rows, cols], 0).astype(BF16)
                 cc = jnp.where(inside, cb[rows, cols], 0).astype(BF16)
-                place_t = begin + lax.broadcasted_iota(jnp.int32, (HALF_T, n), 0)
-                place_s = lax.broadcasted_iota(jnp.int32, (HALF_T, n), 1)
-                allowed = (start_col[rows, 0:1] == start_row[0:1, 0:n]) & (place_s <= place_t)
-                scores = jnp.where(allowed, nt(qq, kk) * scale, -1e30)
+                scores = nt(qq, kk) + bias[rows, 0:n]
                 powers = jnp.exp(scores - jnp.max(scores, axis=-1, keepdims=True))
-                probs = powers / jnp.sum(powers, axis=-1, keepdims=True)
+                probs = powers * (1.0 / jnp.sum(powers, axis=-1, keepdims=True))
                 low = probs.astype(BF16)
                 outs.append(nn(low, vv))
                 back = nt(cc, vv)
                 inner = jnp.sum(probs * back, axis=-1, keepdims=True)
                 ds = (probs * (back - inner)).astype(BF16)
                 grads_q.append(nn(ds, kk) * scale)
-                grads_k.append(tn(ds, qq) * scale)
+                grads_k.append(tn(ds, qq))
                 grads_v.append(tn(low, cc))
             join = lambda parts: jnp.concatenate([parts[1][:HALF_T] + parts[0], parts[1][HALF_T:]], axis=0)
             halves.append(
@@ -538,71 +737,83 @@
     gather.done(1)
     reduce.start(0)
 
-    for half in range(2):
-        base = W_UNITS[half]
-        lane = 5 * D + 1152 + half * 768
-
-        def units(i, carry, base=base, lane=lane):
-            cols = span(i * 256, 256)
-            pre = nn(s2[...], wcols(base + i * 256, 256)) + rowvec(lane + i * 256, 256)
+    own = me.t * HALF_T
+    other = pl.ds(pl.multiple_of((1 - me.t) * HALF_T, HALF_T), HALF_T)
+
+    def units(half):
+        def body(i, carry):
+            cols = span(half * 768 + i * 256, 256)
+            lane = 5 * D + 1152 + half * 768 + i * 256
+            pre = nn(s2[...], wcols(W_UNITS[half] + i * 256, 256)) + rowvec(lane, 256)
             phi = 0.5 * (1.0 + lax.erf(pre * (1.0 / math.sqrt(2.0))))
             act[:, cols] = (pre * phi).astype(BF16)
-            slope = phi + pre * jnp.exp(-0.5 * pre * pre) * (1.0 / math.sqrt(2.0 * math.pi))
-            back = (nn(up[...], wcols(base + 768 + i * 256, 256)) * slope).astype(BF16)
+            slope[:, cols] = phi + pre * jnp.exp(-0.5 * pre * pre) * (1.0 / math.sqrt(2.0 * math.pi))
+            return carry
+
+        lax.fori_loop(0, 3, body, 0)
+
+    def units_back(half):
+        def body(i, carry):
+            cols = span(half * 768 + i * 256, 256)
+            back = (nn(up[...], wcols(W_UNITS[half] + 768 + i * 256, 256)) * slope[:, cols]).astype(BF16)
             ub[:, cols] = back
-            gvec[0:1, span(lane + i * 256, 256)] = jnp.sum(back.astype(F32), axis=0, keepdims=True)
+            lane = 5 * D + 1152 + half * 768 + i * 256
+            gvec[0:1, span(lane, 256)] = jnp.sum(back.astype(F32), axis=0, keepdims=True)
             return carry
 
-        lax.fori_loop(0, 3, units, 0)
-        if half == 0:
-            reduce.turn(0)
-        else:
-            reduce.done(0, pick_t, quad_out)
-            reduce.turn(1)
+        lax.fori_loop(0, 3, body, 0)
+
+    def grads(half):
+        cols = slice(768 * half, 768 * half + 768)
         for i in range(2):
             rows = slice(384 * i, 384 * i + 384)
-            put(i, G_INNER[half], nn(s2t[rows, :], ub[...]))
-            put(i, G_OUTER[half], nn(upt[rows, :], act[...]))
-        if half == 0:
-            for part in range(2):
-                reduce.pull(1, part)
-        else:
-            reduce.pull(2, 0)
-        for i in range(2):
-            rows = slice(384 * i, 384 * i + 384)
-            outp[:, rows] += nt(act[...], wrows(i, base + 768, 768))
-            second = nt(ub[...], wrows(i, base, 768))
-            if half == 0:
-                sec[:, rows] = second
-            else:
-                second += sec[:, rows]
-                nbp[:, rows] += second * vec[0:1, D + 384 * i : D + 384 * i + 384]
-                gvec[0:1, D + 384 * i : D + 384 * i + 384] = jnp.sum(second * hat[:, rows], axis=0, keepdims=True)
-                gvec[0:1, 3 * D + 384 * i : 3 * D + 384 * i + 384] = jnp.sum(second, axis=0, keepdims=True)
-        if half == 0:
-            gather.done(2)
-            reduce.finish(0)
-            reduce.start(1)
-
+            put(i, G_INNER[half], nn(s2t[rows, :], ub[:, cols]))
+            put(i, G_OUTER[half], nn(upt[rows, :], act[:, cols]))
+        for part in range(2):
+            reduce.pull(1 + half, part)
+
+    units(0)
+    reduce.turn(0)
+    gather.done(2)
+    units(1)
+    for i in range(2):
+        rows = slice(384 * i, 384 * i + 384)
+        outp[:, rows] += nt(act[:, 0:768], wrows(i, W_UNITS[0] + 768, 768))
+        outp[:, rows] += nt(act[:, 768:1536], wrows(i, W_UNITS[1] + 768, 768))
+    out_send[...] = outp[other, :].astype(BF16)
+    swap(2, out_send, out_land)
+    reduce.finish(0)
+    units_back(0)
+    grads(0)
+    units_back(1)
+    reduce.start(1)
+    grads(1)
+    reduce.done(0, pick_t, quad_out)
+    reduce.deliver(0, quad_out, quad_land, qs, qr)
+    reduce.turn(1)
+    for i in range(2):
+        rows = slice(384 * i, 384 * i + 384)
+        second = nt(ub[:, 0:768], wrows(i, W_UNITS[0], 768)) + nt(ub[:, 768:1536], wrows(i, W_UNITS[1], 768))
+        nbp[:, rows] += second * vec[0:1, D + 384 * i : D + 384 * i + 384]
+        gvec[0:1, D + 384 * i : D + 384 * i + 384] = jnp.sum(second * hat[:, rows], axis=0, keepdims=True)
+        gvec[0:1, 3 * D + 384 * i : 3 * D + 384 * i + 384] = jnp.sum(second, axis=0, keepdims=True)
+    nb_send[...] = nbp[other, :].astype(BF16)
+    swap(3, nb_send, nb_land)
+    reduce.start(2)
     tile = jnp.zeros((64, 128), F32)
     for begin in range(0, VEC, D):
         width = min(D, VEC - begin)
         cols = slice(begin, begin + width)
         tile += nt((gvec[0:1, cols] * mask[:, cols].astype(F32)).astype(BF16), spread[:, cols])
-    tile = nn(rows_at[...], tile.astype(BF16)).astype(BF16)
-    g[:, :, :, G_SMALL : G_SMALL + 128] = tile.reshape(Y, Z, BLK, 128)
-    g[:, :, :, COLS - 128 : COLS] = jnp.zeros((Y, Z, BLK, 128), BF16)
-    reduce.pull(2, 1)
-    reduce.start(2)
-
-    own = me.t * HALF_T
-    other = pl.ds(pl.multiple_of((1 - me.t) * HALF_T, HALF_T), HALF_T)
-    out_send[...] = outp[other, :].astype(BF16)
-    nb_send[...] = nbp[other, :].astype(BF16)
-    for i, (src, dst) in enumerate(((out_send, out_land), (nb_send, nb_land))):
-        swaps.append(Copy(lambda src=src, dst=dst, i=i: (src, dst, ts.at[2 + i], tr.at[2 + i], partner)))
+    small_mine[...] = nn(rows_at[...], tile.astype(BF16)).reshape(Y, Z, 8, 128)
+    minor.start()
     reduce.finish(1)
     reduce.turn(2)
+    minor.turn()
+    reduce.done(1, pick_t, quad_out)
+    reduce.deliver(1, quad_out, quad_land, qs, qr)
+    minor.finish()
+    reduce.finish(2)
     for copy in swaps[2:]:
         copy.wait_recv()
 
@@ -622,64 +833,24 @@
         return carry
 
     lax.fori_loop(0, 4, finish_rows, 0)
-    reduce.done(1, pick_t, quad_out)
-    reduce.finish(2)
     reduce.done(2, pick_t, quad_out)
-    owners = []
-    for r in (1, 2, 3):
-
-        def parts(r=r):
-            device, xh, c = me.quad(r)
-            return quad_out.at[xh * 2 + c], quad_land.at[me.slot], qs.at[1, r], qr.at[1, r], device
-
-        owners.append(Copy(parts))
-    quad_land[me.slot] = quad_out[me.slot]
-    for copy in owners:
+    reduce.deliver(2, quad_out, quad_land, qs, qr)
+    small_out[...] = minor.done()
+    for copy in reduce.delivered.values():
         copy.wait_recv()
-    small_mine[...] = quad_land[0, :, WIDE - 128 :].astype(F32) + quad_land[2, :, WIDE - 128 :].astype(F32)
-    last = Copy(lambda: (small_mine, small_land, es, er, partner))
     for c in range(2):
         rows_out[c] = quad_land[c].astype(F32) + quad_land[2 + c].astype(F32)
-    for copy in quads + swaps + owners:
+    for copy in list(quads.values()) + swaps:
         copy.wait_send()
     gather.sent()
     reduce.sent()
-    last.wait_send()
-    last.wait_recv()
-    lane = lax.broadcasted_iota(jnp.int32, (PAD, 128), 1)
-    small_out[...] = small_mine[...] + jnp.where(lane < 4 * OWN, small_land[...], 0.0)
-
-
-def turn_tables(starts):
-    places = (jnp.arange(T, dtype=jnp.int32) - starts).astype(F32)
-    lane = jnp.arange(128, dtype=jnp.int32) % HD
-    freqs = jnp.exp((lane % 8).astype(F32) * (-2.0 * math.log(10000.0) / ROT))
-    turns = places[:, None] * freqs[None, :]
-    cosine, sine = jnp.cos(turns), jnp.sin(turns)
-    return (
-        jnp.where(lane < ROT, cosine, 1.0),
-        jnp.where(lane < 8, -sine, 0.0),
-        jnp.where((lane >= 8) & (lane < ROT), sine, 0.0),
-    )
+    minor.sent()
 
 
 def local(
     layer_input, segment_starts, norm_gains, norm_shifts, projection, triple_bias, dense_weight, inner_weight,
     unit_bias, outer_weight, final_bias, cotangent,
 ):
-    small = jnp.concatenate(
-        [norm_gains.reshape(-1), norm_shifts.reshape(-1), final_bias, triple_bias.reshape(-1), unit_bias]
-    )
-    small = jnp.pad(small[None, :], ((0, OWN - 1), (0, 128 - small.shape[0])))
-    triple = projection.reshape(OWN, 1152)
-    mine = jnp.concatenate(
-        [triple[:, :896], inner_weight, triple[:, 896:], small, dense_weight.T, jnp.zeros((OWN, 128), BF16), outer_weight.T],
-        axis=1,
-    )
-    mine = jnp.pad(mine, ((0, PAD - OWN), (0, 0)))
-    mine = jnp.stack([mine[:, :WIDE], mine[:, WIDE:]])
-    start_col = jnp.broadcast_to(segment_starts[:, None], (T, 128))
-    start_row = jnp.broadcast_to(segment_starts[None, :], (8, T))
     vm = pl.BlockSpec(memory_space=pltpu.VMEM)
     dma = pltpu.SemaphoreType.DMA
     struct = jax.ShapeDtypeStruct
@@ -687,57 +858,55 @@
     out, grad, small_grad, rows_grad = pl.pallas_call(
         kernel,
         out_shape=(
-            struct((HALF_T, D), BF16), struct((HALF_T, D), BF16), struct((PAD, 128), F32), struct((2, PAD, WIDE), F32),
+            struct((HALF_T, D), BF16), struct((HALF_T, D), BF16), struct((8, 128), F32), struct((2, PAD, G_WIDE), F32),
         ),
-        in_specs=[vm] * 15,
+        in_specs=[vm] * 19,
         out_specs=(vm,) * 4,
         scratch_shapes=[
-            vmem((Y, Z, BLK, COLS), BF16), vmem((Y, Z, BLK, COLS), BF16), vmem((Y, Z, BLK, WIDE), BF16),
-            vmem((4, BLK, WIDE), BF16), vmem((2, 4, BLK, WIDE), BF16), vmem((3, BLK, WIDE), BF16),
-            vmem((4, PAD, WIDE), BF16), vmem((4, PAD, WIDE), BF16), vmem((4, PAD, WIDE), BF16),
+            vmem((Y, Z, BLK, COLS), BF16), vmem((Y, Z, BLK, G_COLS), BF16), vmem((Y, Z, BLK, G_WIDE), BF16),
+            vmem((4, BLK, G_WIDE), BF16), vmem((2, 4, BLK, G_WIDE), BF16), vmem((3, BLK, G_WIDE), BF16),
+            vmem((4, PAD, WIDE), BF16), vmem((4, PAD, G_WIDE), BF16), vmem((4, PAD, G_WIDE), BF16),
         ]
         + [vmem((HALF_T, D), BF16)] * 6
-        + [vmem((PAD, 128), F32)] * 2
+        + [vmem((Y, Z, 8, 128), F32), vmem((4, 4, 8, 128), F32), vmem((4, 8, 128), F32), vmem((8, 8, 128), F32)]
         + [vmem((T, D), BF16)] * 3
         + [vmem((D, T), BF16)] * 3
         + [vmem((T, D), F32), vmem((T, 128), F32)]
         + [vmem((T, 384), BF16)] * 5
-        + [vmem((T, 1152), BF16), vmem((T, 768), BF16), vmem((T, 768), BF16)]
-        + [vmem((T, D), F32)] * 3
+        + [vmem((T, 1152), BF16), vmem((T, 1536), BF16), vmem((T, 1536), BF16)]
+        + [vmem((T, D), F32)] * 2
         + [vmem((8, VEC), F32)] * 2
+        + [vmem((2, PAD, WIDE), BF16)]
+        + [vmem((T, 128), F32)] * 3
+        + [vmem((T, T), F32), vmem((T, 1536), F32)]
         + [dma((3, 2, 3))] * 2
+        + [dma((3, 2, 6))] * 2
         + [dma((3, 2, 4))] * 4
-        + [dma((3, 2, 4))] * 4
+        + [dma((3, 2, 6))] * 2
         + [dma((3, 2, 3))] * 2
-        + [dma((2, 4))] * 2
+        + [dma((2, 3, 4))] * 2
         + [dma((4,))] * 2
-        + [dma] * 2,
+        + [dma((13,))] * 2,
         compiler_params=pltpu.CompilerParams(collective_id=0, has_side_effects=True, vmem_limit_bytes=VMEM_LIMIT),
         name="layer",
     )(
-        mine, layer_input, cotangent, *[jnp.asarray(m) for m in order_tables()], *turn_tables(segment_starts),
-        start_col, start_row,
+        projection.reshape(OWN, 1152), dense_weight.T, inner_weight, outer_weight.T, norm_gains, norm_shifts,
+        final_bias.reshape(1, OWN), triple_bias, unit_bias.reshape(1, 24), segment_starts.reshape(1, T),
+        layer_input, cotangent, *[jnp.asarray(m) for m in order_tables()],
     )
-
-    vals = small_grad[0]
-    side = lax.axis_index("tensor")
-
-    def six(field):
-        return lax.dynamic_slice_in_dim(field, side * 6, 6, axis=field.ndim - 1)
-
-    a, b = rows_grad[0, :OWN], rows_grad[1, :OWN]
+    gains, shifts, triple_b, units, final, proj, dense, inner, outer = pl.pallas_call(
+        unpack_kernel,
+        out_shape=(
+            struct((2, 6), F32), struct((2, 6), F32), struct((3, 6), F32), struct((1, 24), F32), struct((1, 6), F32),
+            struct((OWN, 1152), F32), struct((OWN, 384), F32), struct((OWN, 1536), F32), struct((OWN, 1536), F32),
+        ),
+        in_specs=[vm] * 2,
+        out_specs=(vm,) * 9,
+        name="unpack",
+    )(rows_grad, small_grad)
     return (
-        out,
-        grad,
-        six(vals[0:24].reshape(2, OWN)),
-        six(vals[24:48].reshape(2, OWN)),
-        jnp.concatenate([a[:, :768], b[:, :384]], axis=1).reshape(OWN, 3, 384),
-        vals[OFF_TB:OFF_UB].reshape(3, 6),
-        b[:, 384:768].T,
-        a[:, 768:2304],
-        vals[OFF_UB : OFF_UB + 24],
-        b[:, 768:2304].T,
-        six(vals[48:60]),
+        out, grad, gains, shifts, proj.reshape(OWN, 3, 384), triple_b, dense.T, inner, units.reshape(24), outer.T,
+        final.reshape(6),
     )
 
 

time: 144 us -> 107 us (0.74)
  Pallas kernels: 120 us -> 99.3 us
  local copies, waits for them, and re-layouts: 19 us -> 6.48 us
  other arithmetic: 3.28 us -> 0 us
    pallas_call x1, Pallas kernels: 120 us -> 97.1 us  [local(): pl.pallas_call(kernel, out_shape=(struct((HALF_T, D), BF16), struct((HALF...]
    slice x5 -> x0, local copies, waits for them, and re-layouts: 3.55 us -> none  [the longest x1 1.38 us: local(): vals[24:48].reshape(2, OWN)]
    concatenate x2 -> x0, local copies, waits for them, and re-layouts: 2.23 us -> none  [the longest x1 1.43 us: local(): jnp.concatenate([norm_gains.reshape(-1), norm_shifts.reshape(-1), final_b...]
    reshape x7 -> x1, local copies, waits for them, and re-layouts: 3.72 us -> 1.54 us  [local(): proj.reshape(OWN, 3, 384)]
    pallas_call x0 -> x1, Pallas kernels: none -> 2.13 us  [local(): pl.pallas_call(unpack_kernel, out_shape=(struct((2, 6), F32), struct((2,...]
    select_n x1 -> x0, other arithmetic: 1.88 us -> none  [turn_tables(): jnp.where((lane >= 8) & (lane < ROT), sine, 0.0)]
    dynamic_slice x3 -> x0, local copies, waits for them, and re-layouts: 1.85 us -> none  [six(): return lax.dynamic_slice_in_dim(field, side * 6, 6, axis=field.ndim - 1)]
    broadcast_in_dim x2 -> x0, local copies, waits for them, and re-layouts: 1.46 us -> none  [the longest x1 0.85 us: local(): start_col = jnp.broadcast_to(segment_starts[:, None], (T, 128))]
where the time goes in v3:
time: 107 us; the launch traced here: 106 us
  Pallas kernels  99.3 us (93%)
  local copies, waits for them, and re-layouts  6.48 us (6%)
    pallas_call x1, Pallas kernels, local(): pl.pallas_call(kernel, out_shape=(struct((HALF_T, D), BF16), struct((HALF...  97.1 us
    unnamed x4, local copies, waits for them, and re-layouts  4.94 us

profile of v3, /device:TPU:1, one launch (start us, length us, event | category | flops | bytes accessed | tf_op | source)
XLA Modules:
  0.0 106.4 jit_solution(6684022852750023937)
XLA Ops:
  0.6 0.8 pad
  1.4 0.6 copy.30
  2.1 97.1 %layer.1 = (bf16[256,768]{1,0:T(8,128)(2,1)}, bf16[256,768]{1,0:T(8,128)(2,1)}, f32[8,128]{1,0:T(8,128)}, f32[2,16,2304]{2,1,0:T(8,128)}) custom-call(bf16[12,1152]{1,0:T(8,128)(2,1)} %bitcast.13, bf16[12,384]{1,0:T(8,128)(2,1)} %bitcast.15, bf16[12,1536]{1,0:T(8,128)(2,1)} %inner_w.1, bf16[12,1536]{1,0:T(8,128)(2,1)} %bitcast.14, bf16[2,12]{1,0:T(2,128)(2,1)} %gains.1, ...), custom_call_target="tpu_custom_call" | custom-call | tf_op jit(solution)/shard_map/layer/pallas_call | solution.py:858
  99.2 2.1 %unpack.1 = (f32[2,6]{1,0:T(2,128)}, f32[2,6]{1,0:T(2,128)}, f32[3,6]{1,0:T(4,128)}, f32[1,24]{1,0:T(1,128)}, f32[1,6]{1,0:T(1,128)}, /*index=5*/f32[12,1152]{1,...) custom-call(f32[2,16,2304]{2,1,0:T(8,128)} %get-tuple-element.26.rows, f32[8,128]{1,0:T(8,128)} %get-tuple-element.27.small), custom_call_target="tpu_custom_call" | custom-call | tf_op jit(solution)/shard_map/unpack/pallas_call | solution.py:897
  101.3 1.5 %reshape.47 = f32[12,3,384]{2,1,0:T(4,128)} reshape(f32[12,1152]{1,0:T(8,128)} %get-tuple-element.30) | data formatting | bytes 110592 | tf_op jit(solution)/shard_map/reshape | solution.py:908
  102.9 1.8 %copy.33 = bf16[256,768]{1,0:T(8,128)(2,1)} copy(bf16[256,768]{1,0:T(8,128)(2,1)} %get-tuple-element.48) | data formatting | bytes 786432
  104.6 1.8 %copy.34 = bf16[256,768]{1,0:T(8,128)(2,1)} copy(bf16[256,768]{1,0:T(8,128)(2,1)} %get-tuple-element.49) | data formatting | bytes 786432

commit v4 on v3

--- a/solution.py
+++ b/solution.py
@@ -113,11 +113,12 @@
         return out + [self.other(r) for r in range(4)]
 
 
-def enter(place):
+def enter(place, beside):
     barrier = pltpu.get_barrier_semaphore()
     peers = place.peers()
     for peer in peers:
         pl.semaphore_signal(barrier, inc=1, device_id=peer, device_id_type=MESH)
+    beside()
     pl.semaphore_wait(barrier, len(peers))
 
 
@@ -456,7 +457,7 @@
     return jnp.where(test(row, col), 1.0, 0.0)
 
 
-def pack(triple, dense, inner, outer, small, mine):
+def pack(triple, dense, inner, outer, small, mine, rows):
     mine[...] = jnp.zeros_like(mine)
     tall = one_hot((PAD, OWN), lambda r, c: r == c).astype(BF16)
     line = jnp.zeros((1, 128), F32)
@@ -468,10 +469,14 @@
             line += nn(ref[i : i + 1, :], put)
             begin += width
     first = lax.broadcasted_iota(jnp.int32, (PAD, 128), 0) == 0
-    rows = nn(tall, triple[...]).astype(BF16)
-    mine[0, :, 0:896] = rows[:, 0:896]
+    rows[...] = jnp.zeros_like(rows)
+    for r in range(OWN):
+        line3 = triple[r].astype(F32)
+        for n in range(3):
+            rows[r : r + 1, 384 * n : 384 * n + 384] = line3[n : n + 1, :]
+    mine[0, :, 0:896] = rows[:, 0:896].astype(BF16)
     mine[0, :, 896:WIDE] = nn(tall, inner[...]).astype(BF16)
-    mine[1, :, 0:256] = rows[:, 896:1152]
+    mine[1, :, 0:256] = rows[:, 896:1152].astype(BF16)
     mine[1, :, 256:384] = jnp.where(first, line, 0.0).astype(BF16)
     mine[1, :, 384:768] = nn(tall, dense[...]).astype(BF16)
     mine[1, :, 896:WIDE] = nn(tall, outer[...]).astype(BF16)
@@ -508,7 +513,11 @@
     lax.fori_loop(0, 4, body, 0)
 
 
-def unpack_kernel(rows, small, gains, shifts, triple_b, units, final, proj, dense, inner, outer):
+def unpack_kernel(
+    rows, small, out_in, grad_in, gains, shifts, triple_b, units, final, proj, dense, inner, outer, out, grad
+):
+    out[...] = out_in[...]
+    grad[...] = grad_in[...]
     side = lax.axis_index("tensor")
     line = jnp.broadcast_to(small[0:1, :], (8, 128))
 
@@ -526,8 +535,8 @@
         triple_b[i : i + 1, :] = lanes(OFF_TB + 6 * i, 6)
     units[...] = lanes(OFF_UB, 24)
     final[...] = lanes(4 * OWN + side * 6, 6)
-    proj[:, 0:768] = rows[0, 0:OWN, 0:768]
-    proj[:, 768:1152] = rows[1, 0:OWN, 0:384]
+    for n in range(3):
+        proj[:, n, :] = rows[0, 0:OWN, 384 * n : 384 * n + 384] if n < 2 else rows[1, 0:OWN, 0:384]
     inner[...] = rows[0, 0:OWN, 768:2304]
     dense[...] = rows[1, 0:OWN, 384:768]
     outer[...] = rows[1, 0:OWN, 768:2304]
@@ -540,12 +549,11 @@
     w, g, land, ring1, ring2, red, quad_in, quad_out, quad_land, x_land, cot_land, out_send, out_land, nb_send, nb_land,
     small_mine, small_z, small_y, small_q,
     s1, s2, up, s1t, s2t, upt, hat, fac, q, k, v, cb, ctx, tb, act, ub, outp, nbp, vec, gvec,
-    mine, cos_t, left_t, right_t, bias, slope,
+    mine, cos_t, left_t, right_t, bias, slope, rows_in,
     ap0s, ap0r, ap1s, ap1r, ass, asr, rcs, rcr, rp0s, rp0r, rp1s, rp1r, qs, qr, ts, tr, es, er,
 ):
     me = Place()
-    pack(triple, dense, inner_w, outer_w, (gains, shifts, fbias, tbias, ubias), mine)
-    enter(me)
+    enter(me, lambda: pack(triple, dense, inner_w, outer_w, (gains, shifts, fbias, tbias, ubias), mine, rows_in))
     partner = me.dev(t=1 - me.t)
     gather = Gather(me, w, (ap0s, ap0r, ap1s, ap1r, ass, asr))
     reduce = Reduce(me, g, land, ring1, ring2, red, (rcs, rcr, rp0s, rp0r, rp1s, rp1r))
@@ -580,27 +588,29 @@
     block(0)
     swap(1, cot, cot_land)
     def norm_rows(x_ref, first_row):
+        rows = pl.ds(pl.multiple_of(first_row, HALF_T), HALF_T)
+        hat[rows, :] = nn(x_ref[...], perm[...])
+
         def body(i, carry):
-            src = pl.ds(pl.multiple_of(i * 128, 128), 128)
-            rows = pl.ds(pl.multiple_of(first_row + i * 128, 128), 128)
-            field = nn(x_ref[src, :], perm[...])
-            center = jnp.mean(field, axis=-1, keepdims=True)
-            centred = field - center
+            at = pl.ds(pl.multiple_of(first_row + i * 64, 64), 64)
+            field = hat[at, :]
+            centred = field - jnp.mean(field, axis=-1, keepdims=True)
             factor = lax.rsqrt(jnp.mean(centred * centred, axis=-1, keepdims=True) + EPSILON)
-            hat[rows, :] = centred * factor
-            fac[rows, :] = jnp.broadcast_to(factor, (128, 128))
+            hat[at, :] = centred * factor
+            fac[at, :] = jnp.broadcast_to(factor, (64, 128))
             return carry
 
-        lax.fori_loop(0, 2, body, 0)
+        lax.fori_loop(0, 4, body, 0)
 
     def back_rows(cot_ref, first_row):
+        rows = pl.ds(pl.multiple_of(first_row, HALF_T), HALF_T)
+        up[rows, :] = nn(cot_ref[...], perm[...]).astype(BF16)
+
         def body(i, carry):
-            src = pl.ds(pl.multiple_of(i * 128, 128), 128)
-            rows = pl.ds(pl.multiple_of(first_row + i * 128, 128), 128)
-            upstream = nn(cot_ref[src, :], perm[...])
-            up[rows, :] = upstream.astype(BF16)
-            upt[:, rows] = upstream.astype(BF16).T
-            gvec[0:1, 4 * D : 5 * D] += jnp.sum(upstream, axis=0, keepdims=True)
+            at = pl.ds(pl.multiple_of(first_row + i * 128, 128), 128)
+            upstream = up[at, :]
+            upt[:, at] = upstream.T
+            gvec[0:1, 4 * D : 5 * D] += jnp.sum(upstream.astype(F32), axis=0, keepdims=True)
             return carry
 
         lax.fori_loop(0, 2, body, 0)
@@ -608,8 +618,8 @@
     norm_rows(x, me.t * HALF_T)
     gather.turn(0)
     back_rows(cot, me.t * HALF_T)
+    gather.forward(0)
     block(1)
-    gather.forward(0)
     swaps[0].wait_recv()
     norm_rows(x_land, (1 - me.t) * HALF_T)
     gather.finish(0)
@@ -651,23 +661,21 @@
         return carry
 
     lax.fori_loop(0, 4, scale_rows, 0)
+
+    scale = 1.0 / math.sqrt(HD)
+
+    def thrice(table):
+        return jnp.concatenate([table[...]] * 3, axis=1)
+
+    for n, ref in enumerate((q, k, v)):
+        field = nn(s1[...], wcols(n * 384, 384)) + rowvec(5 * D + n * 384, 384)
+        if n < 2:
+            field = rotated(field, thrice(cos_t), thrice(left_t), thrice(right_t), 1.0)
+        field = field.astype(BF16)
+        ref[...] = field * BF16(scale) if n == 0 else field
     swaps[1].wait_recv()
     back_rows(cot_land, (1 - me.t) * HALF_T)
-
-    scale = 1.0 / math.sqrt(HD)
-
-    def heads_in(i, carry):
-        cols = span(i * 128, 128)
-        for n, ref in enumerate((q, k, v)):
-            field = nn(s1[...], wcols(n * 384 + i * 128, 128)) + rowvec(5 * D + n * 384 + i * 128, 128)
-            if n < 2:
-                field = rotated(field, cos_t[...], left_t[...], right_t[...], 1.0)
-            field = field.astype(BF16)
-            ref[:, cols] = field * BF16(scale) if n == 0 else field
-        cb[:, cols] = nn(up[...], wcols(W_DENSE + i * 128, 128)).astype(BF16)
-        return carry
-
-    lax.fori_loop(0, 3, heads_in, 0)
+    cb[...] = nn(up[...], wcols(W_DENSE, 384)).astype(BF16)
     gather.forward(1)
 
     def attend(pair, carry):
@@ -730,12 +738,7 @@
     for i in range(2):
         rows = slice(384 * i, 384 * i + 384)
         outp[:, rows] = nt(ctx[...], wrows(i, W_DENSE, 384))
-        first = nt(tb[...], wrows(i, 0, 1152))
-        nbp[:, rows] = first * vec[0:1, rows]
-        gvec[0:1, rows] = jnp.sum(first * hat[:, rows], axis=0, keepdims=True)
-        gvec[0:1, slice(2 * D + 384 * i, 2 * D + 384 * i + 384)] = jnp.sum(first, axis=0, keepdims=True)
     gather.done(1)
-    reduce.start(0)
 
     own = me.t * HALF_T
     other = pl.ds(pl.multiple_of((1 - me.t) * HALF_T, HALF_T), HALF_T)
@@ -773,7 +776,7 @@
             reduce.pull(1 + half, part)
 
     units(0)
-    reduce.turn(0)
+    reduce.start(0)
     gather.done(2)
     units(1)
     for i in range(2):
@@ -782,24 +785,27 @@
         outp[:, rows] += nt(act[:, 768:1536], wrows(i, W_UNITS[1] + 768, 768))
     out_send[...] = outp[other, :].astype(BF16)
     swap(2, out_send, out_land)
-    reduce.finish(0)
     units_back(0)
+    reduce.turn(0)
     grads(0)
     units_back(1)
+    reduce.finish(0)
     reduce.start(1)
     grads(1)
+    for i in range(2):
+        rows = slice(384 * i, 384 * i + 384)
+        first = nt(tb[...], wrows(i, 0, 1152))
+        second = nt(ub[:, 0:768], wrows(i, W_UNITS[0], 768)) + nt(ub[:, 768:1536], wrows(i, W_UNITS[1], 768))
+        nbp[:, rows] = first * vec[0:1, rows] + second * vec[0:1, D + 384 * i : D + 384 * i + 384]
+        normal = hat[:, rows]
+        for n, term in enumerate((first * normal, second * normal, first, second)):
+            gvec[0:1, n * D + 384 * i : n * D + 384 * i + 384] = jnp.sum(term, axis=0, keepdims=True)
+    nb_send[...] = nbp[other, :].astype(BF16)
+    swap(3, nb_send, nb_land)
+    reduce.start(2)
     reduce.done(0, pick_t, quad_out)
     reduce.deliver(0, quad_out, quad_land, qs, qr)
     reduce.turn(1)
-    for i in range(2):
-        rows = slice(384 * i, 384 * i + 384)
-        second = nt(ub[:, 0:768], wrows(i, W_UNITS[0], 768)) + nt(ub[:, 768:1536], wrows(i, W_UNITS[1], 768))
-        nbp[:, rows] += second * vec[0:1, D + 384 * i : D + 384 * i + 384]
-        gvec[0:1, D + 384 * i : D + 384 * i + 384] = jnp.sum(second * hat[:, rows], axis=0, keepdims=True)
-        gvec[0:1, 3 * D + 384 * i : 3 * D + 384 * i + 384] = jnp.sum(second, axis=0, keepdims=True)
-    nb_send[...] = nbp[other, :].astype(BF16)
-    swap(3, nb_send, nb_land)
-    reduce.start(2)
     tile = jnp.zeros((64, 128), F32)
     for begin in range(0, VEC, D):
         width = min(D, VEC - begin)
@@ -817,11 +823,12 @@
     for copy in swaps[2:]:
         copy.wait_recv()
 
+    low = nn(x[...], perm[...]) + outp[pl.ds(pl.multiple_of(own, HALF_T), HALF_T), :] + out_land[...].astype(F32) + fb
+    out[...] = nt(low.astype(BF16), perm[...]).astype(BF16)
+
     def finish_rows(i, carry):
         rows = pl.ds(pl.multiple_of(i * 64, 64), 64)
         mine_at = pl.ds(pl.multiple_of(own + i * 64, 64), 64)
-        low = (nn(x[rows, :], perm[...]) + outp[mine_at, :] + out_land[rows, :].astype(F32) + fb).astype(BF16)
-        out[rows, :] = nt(low, perm[...]).astype(BF16)
         back = nbp[mine_at, :] + nb_land[rows, :].astype(F32)
         normal = hat[mine_at, :]
         value = up[mine_at, :].astype(F32) + fac[mine_at, 0:1] * (
@@ -829,10 +836,11 @@
             - jnp.mean(back, axis=-1, keepdims=True)
             - normal * jnp.mean(back * normal, axis=-1, keepdims=True)
         )
-        grad[rows, :] = nt(value.astype(BF16), perm[...]).astype(BF16)
+        x_land[rows, :] = value.astype(BF16)
         return carry
 
     lax.fori_loop(0, 4, finish_rows, 0)
+    grad[...] = nt(x_land[...], perm[...]).astype(BF16)
     reduce.done(2, pick_t, quad_out)
     reduce.deliver(2, quad_out, quad_land, qs, qr)
     small_out[...] = minor.done()
@@ -878,7 +886,7 @@
         + [vmem((8, VEC), F32)] * 2
         + [vmem((2, PAD, WIDE), BF16)]
         + [vmem((T, 128), F32)] * 3
-        + [vmem((T, T), F32), vmem((T, 1536), F32)]
+        + [vmem((T, T), F32), vmem((T, 1536), F32), vmem((PAD, 1152), F32)]
         + [dma((3, 2, 3))] * 2
         + [dma((3, 2, 6))] * 2
         + [dma((3, 2, 4))] * 4
@@ -890,22 +898,23 @@
         compiler_params=pltpu.CompilerParams(collective_id=0, has_side_effects=True, vmem_limit_bytes=VMEM_LIMIT),
         name="layer",
     )(
-        projection.reshape(OWN, 1152), dense_weight.T, inner_weight, outer_weight.T, norm_gains, norm_shifts,
+        projection, dense_weight.T, inner_weight, outer_weight.T, norm_gains, norm_shifts,
         final_bias.reshape(1, OWN), triple_bias, unit_bias.reshape(1, 24), segment_starts.reshape(1, T),
         layer_input, cotangent, *[jnp.asarray(m) for m in order_tables()],
     )
-    gains, shifts, triple_b, units, final, proj, dense, inner, outer = pl.pallas_call(
+    gains, shifts, triple_b, units, final, proj, dense, inner, outer, out, grad = pl.pallas_call(
         unpack_kernel,
         out_shape=(
             struct((2, 6), F32), struct((2, 6), F32), struct((3, 6), F32), struct((1, 24), F32), struct((1, 6), F32),
-            struct((OWN, 1152), F32), struct((OWN, 384), F32), struct((OWN, 1536), F32), struct((OWN, 1536), F32),
+            struct((OWN, 3, 384), F32), struct((OWN, 384), F32), struct((OWN, 1536), F32), struct((OWN, 1536), F32),
+            struct((HALF_T, D), BF16), struct((HALF_T, D), BF16),
         ),
-        in_specs=[vm] * 2,
-        out_specs=(vm,) * 9,
+        in_specs=[vm] * 4,
+        out_specs=(vm,) * 11,
         name="unpack",
-    )(rows_grad, small_grad)
+    )(rows_grad, small_grad, out, grad)
     return (
-        out, grad, gains, shifts, proj.reshape(OWN, 3, 384), triple_b, dense.T, inner, units.reshape(24), outer.T,
+        out, grad, gains, shifts, proj, triple_b, dense.T, inner, units.reshape(24), outer.T,
         final.reshape(6),
     )
 

time: 107 us -> 96.2 us (0.90)
  local copies, waits for them, and re-layouts: 6.48 us -> 0 us
  Pallas kernels: 99.3 us -> 95.4 us
    unnamed x4 -> x0, local copies, waits for them, and re-layouts: 4.94 us -> none
    pallas_call x1, Pallas kernels: 97.1 us -> 92.7 us  [local(): pl.pallas_call(kernel, out_shape=(struct((HALF_T, D), BF16), struct((HALF...]
    reshape x1 -> x0, local copies, waits for them, and re-layouts: 1.54 us -> none  [local(): proj.reshape(OWN, 3, 384)]
where the time goes in v4:
time: 96.2 us; the launch traced here: 96 us
  Pallas kernels  95.4 us (99%)
    pallas_call x1, Pallas kernels, local(): pl.pallas_call(kernel, out_shape=(struct((HALF_T, D), BF16), struct((HALF...  92.7 us
    pallas_call x1, Pallas kernels, local(): pl.pallas_call(unpack_kernel, out_shape=(struct((2, 6), F32), struct((2,...  2.68 us

profile of v4, /device:TPU:1, one launch (start us, length us, event | category | flops | bytes accessed | tf_op | source)
XLA Modules:
  0.0 96.0 jit_solution(18001717193547012148)
XLA Ops:
  0.6 92.7 %layer.1 = (bf16[256,768]{1,0:T(8,128)(2,1)}, bf16[256,768]{1,0:T(8,128)(2,1)}, f32[8,128]{1,0:T(8,128)}, f32[2,16,2304]{2,1,0:T(8,128)}) custom-call(bf16[12,3,384]{2,1,0:T(4,128)(2,1)} %triple.1, bf16[12,384]{1,0:T(8,128)(2,1)} %bitcast.10, bf16[12,1536]{1,0:T(8,128)(2,1)} %inner_w.1, bf16[12,1536]{1,0:T(8,128)(2,1)} %bitcast.9, bf16[2,12]{1,0:T(2,128)(2,1)} %gains.1, ...), custom_call_target="tpu_custom_call" | custom-call | tf_op jit(solution)/shard_map/layer/pallas_call | solution.py:866
  93.4 2.7 %unpack.1 = (f32[2,6]{1,0:T(2,128)}, f32[2,6]{1,0:T(2,128)}, f32[3,6]{1,0:T(4,128)}, f32[1,24]{1,0:T(1,128)}, f32[1,6]{1,0:T(1,128)}, /*index=5*/f32[12,3,384]{2...) custom-call(f32[2,16,2304]{2,1,0:T(8,128)} %get-tuple-element.26.row, ...), custom_call_target="tpu_custom_call" | custom-call | tf_op jit(solution)/shard_map/unpack/pallas_call | solution.py:905

commit v5 on v4

--- a/solution.py
+++ b/solution.py
@@ -206,7 +206,8 @@
                 self.onward(group, part, 0, i, i, step)
             for i, step in enumerate((1, 3)):
                 self.onward(group, part, 0, 1 - i, 4 + i, step)
-            self.share(group, part, 0)
+            if group == 0:
+                self.share(group, part, 0)
 
     def forward(self, group):
         for part in range(2):
@@ -218,16 +219,26 @@
         for part in range(2):
             for i, step in enumerate((1, 3)):
                 self.second[group, part, 4 + i].wait_recv()
-                self.share(group, part, 4 - step)
+                if group == 0:
+                    self.share(group, part, 4 - step)
         for part in range(2):
             for i in range(2):
                 self.second[group, part, 2 + i].wait_recv()
-            self.share(group, part, 2)
+            if group == 0:
+                self.share(group, part, 2)
+        if group > 0:
+
+            def parts():
+                base, half, _, _ = W_GROUPS[group]
+                ref = self.w.at[:, :, :, span(self.me.c * half + base, half)]
+                return ref, ref, self.ss.at[group, 0, 0], self.sr.at[group, 0, 0], self.sibling
+
+            self.shared[group, 0, 0] = Copy(parts)
 
     def done(self, group):
-        for part in range(2):
-            for step in range(4):
-                self.shared[group, part, step].wait_recv()
+        for at, copy in self.shared.items():
+            if at[0] == group:
+                copy.wait_recv()
 
     def sent(self):
         for copies in (self.first, self.second, self.shared):
@@ -263,12 +274,11 @@
             return ref.at[lax.rem(self.me.y + step, 4), :, :, cols]
         return ref.at[:, lax.rem(self.me.z + step, 4), :, cols]
 
-    def landed(self, group, part, step):
-        _, at, width = self.place(group, part)
-        return self.of(self.land, part, step, span(at, width))
-
     def add(self, dst, *terms):
         def body(i, carry):
+            if len(terms) == 1:
+                dst[i] = dst[i] + terms[0][i]
+                return carry
             total = dst[i].astype(F32)
             for term in terms:
                 total += term[i].astype(F32)
@@ -277,27 +287,35 @@
 
         lax.fori_loop(0, 4, body, 0)
 
-    def pull(self, group, part):
-        for step in (2, 1, 3, 0):
-
-            def parts(step=step):
-                at = (group, part, step)
-                src = self.unit(group, part, step, core=1 - self.me.c)
-                return src, self.landed(group, part, step), self.cs.at[at], self.cr.at[at], self.sibling
-
-            self.pulled[group, part, step] = Copy(parts)
-
-    def join(self, group, part, step):
-        self.pulled[group, part, step].wait_recv()
-        self.add(self.unit(group, part, step), self.landed(group, part, step))
+    def pull(self, group):
+        base, half, _, at = G_GROUPS[group]
+
+        def parts():
+            src = self.g.at[:, :, :, span((1 - self.me.c) * half + base, half)]
+            dst = self.land.at[:, :, :, span(at, half)]
+            return src, dst, self.cs.at[group], self.cr.at[group], self.sibling
+
+        self.pulled[group] = Copy(parts)
+
+    def join(self, group):
+        self.pulled[group].wait_recv()
+        base, half, _, at = G_GROUPS[group]
+        cols = span(self.me.c * half + base, half)
+
+        def body(i, carry):
+            y, z = lax.div(i, 4), lax.rem(i, 4)
+            self.g[y, z, :, cols] = self.g[y, z, :, cols] + self.land[y, z, :, at : at + half]
+            return carry
+
+        lax.fori_loop(0, 16, body, 0)
 
     def piece1(self, group, part, i):
         _, at, width = self.place(group, part, i)
         return self.ring1.at[:, :, span(at, width)]
 
     def start(self, group):
+        self.join(group)
         for part in range(2):
-            self.join(group, part, 2)
             for i, step in enumerate((1, 3)):
 
                 def parts(part=part, i=i, step=step):
@@ -308,7 +326,6 @@
                 self.first[group, part, i] = Copy(parts)
         for part in range(2):
             for i, step in enumerate((1, 3)):
-                self.join(group, part, step)
                 self.owner(group, part, i, 1 - i, 4 + i, step)
 
     def owner(self, group, part, i, piece, sem, step):
@@ -341,7 +358,6 @@
 
     def finish(self, group):
         for part in range(2):
-            self.join(group, part, 0)
             for i in range(2):
                 self.first[group, part, 4 + i].wait_recv()
                 self.first[group, part, 2 + i].wait_recv()
@@ -521,20 +537,21 @@
     side = lax.axis_index("tensor")
     line = jnp.broadcast_to(small[0:1, :], (8, 128))
 
-    def lanes(begin, width):
-        put = one_hot((128, width), lambda r, c: r == c + begin)
-        picked = lax.dot_general(
-            line, put, (((1,), (0,)), ((), ())), preferred_element_type=F32, precision=lax.Precision.HIGHEST
+    def product(rows_in, put):
+        return lax.dot_general(
+            rows_in, put, (((1,), (0,)), ((), ())), preferred_element_type=F32, precision=lax.Precision.HIGHEST
         )
-        return picked[0:1, :]
-
-    for i in range(2):
-        gains[i : i + 1, :] = lanes(OWN * i + side * 6, 6)
-        shifts[i : i + 1, :] = lanes(2 * OWN + OWN * i + side * 6, 6)
-    for i in range(3):
-        triple_b[i : i + 1, :] = lanes(OFF_TB + 6 * i, 6)
-    units[...] = lanes(OFF_UB, 24)
-    final[...] = lanes(4 * OWN + side * 6, 6)
+
+    row = lax.broadcasted_iota(jnp.int32, (8, 128), 0)
+    lane = lax.broadcasted_iota(jnp.int32, (8, 128), 1)
+    begin = jnp.where(row < 5, 2 * row + side, row + 5) * 6
+    held = jnp.where((lane >= begin) & (lane < begin + 6), line, 0.0)
+    sixes = product(held, one_hot((128, 6), lambda r, c: r % 6 == c))
+    gains[...] = sixes[0:2, :]
+    shifts[...] = sixes[2:4, :]
+    final[...] = sixes[4:5, :]
+    triple_b[...] = sixes[5:8, :]
+    units[...] = product(line, one_hot((128, 24), lambda r, c: r == c + OFF_UB))[0:1, :]
     for n in range(3):
         proj[:, n, :] = rows[0, 0:OWN, 384 * n : 384 * n + 384] if n < 2 else rows[1, 0:OWN, 0:384]
     inner[...] = rows[0, 0:OWN, 768:2304]
@@ -733,8 +750,7 @@
         rows = slice(384 * i, 384 * i + 384)
         put(i, 0, nn(s1t[rows, :], tb[...]))
         put(i, G_DENSE, nn(upt[rows, :], ctx[...]))
-    for part in range(2):
-        reduce.pull(0, part)
+    reduce.pull(0)
     for i in range(2):
         rows = slice(384 * i, 384 * i + 384)
         outp[:, rows] = nt(ctx[...], wrows(i, W_DENSE, 384))
@@ -772,25 +788,24 @@
             rows = slice(384 * i, 384 * i + 384)
             put(i, G_INNER[half], nn(s2t[rows, :], ub[:, cols]))
             put(i, G_OUTER[half], nn(upt[rows, :], act[:, cols]))
-        for part in range(2):
-            reduce.pull(1 + half, part)
+        reduce.pull(1 + half)
 
     units(0)
     reduce.start(0)
+    units_back(0)
+    grads(0)
+    reduce.turn(0)
     gather.done(2)
     units(1)
+    reduce.start(1)
     for i in range(2):
         rows = slice(384 * i, 384 * i + 384)
         outp[:, rows] += nt(act[:, 0:768], wrows(i, W_UNITS[0] + 768, 768))
         outp[:, rows] += nt(act[:, 768:1536], wrows(i, W_UNITS[1] + 768, 768))
     out_send[...] = outp[other, :].astype(BF16)
     swap(2, out_send, out_land)
-    units_back(0)
-    reduce.turn(0)
-    grads(0)
     units_back(1)
     reduce.finish(0)
-    reduce.start(1)
     grads(1)
     for i in range(2):
         rows = slice(384 * i, 384 * i + 384)
@@ -802,10 +817,10 @@
             gvec[0:1, n * D + 384 * i : n * D + 384 * i + 384] = jnp.sum(term, axis=0, keepdims=True)
     nb_send[...] = nbp[other, :].astype(BF16)
     swap(3, nb_send, nb_land)
+    reduce.turn(1)
     reduce.start(2)
     reduce.done(0, pick_t, quad_out)
     reduce.deliver(0, quad_out, quad_land, qs, qr)
-    reduce.turn(1)
     tile = jnp.zeros((64, 128), F32)
     for begin in range(0, VEC, D):
         width = min(D, VEC - begin)
@@ -889,7 +904,8 @@
         + [vmem((T, T), F32), vmem((T, 1536), F32), vmem((PAD, 1152), F32)]
         + [dma((3, 2, 3))] * 2
         + [dma((3, 2, 6))] * 2
-        + [dma((3, 2, 4))] * 4
+        + [dma((3, 2, 4))] * 2
+        + [dma((3,))] * 2
         + [dma((3, 2, 6))] * 2
         + [dma((3, 2, 3))] * 2
         + [dma((2, 3, 4))] * 2

time: 96.2 us -> 95.7 us (level)
  no operation moved by 1% of the time
where the time goes in v5:
time: 95.7 us; the launch traced here: 95.5 us
  Pallas kernels  94.8 us (99%)
    pallas_call x1, Pallas kernels, local(): pl.pallas_call(kernel, out_shape=(struct((HALF_T, D), BF16), struct((HALF...  92.4 us
    pallas_call x1, Pallas kernels, local(): pl.pallas_call(unpack_kernel, out_shape=(struct((2, 6), F32), struct((2,...  2.33 us

profile of v5, /device:TPU:1, one launch (start us, length us, event | category | flops | bytes accessed | tf_op | source)
XLA Modules:
  0.0 95.5 jit_solution(7378454720602114786)
XLA Ops:
  0.6 92.4 %layer.1 = (bf16[256,768]{1,0:T(8,128)(2,1)}, bf16[256,768]{1,0:T(8,128)(2,1)}, f32[8,128]{1,0:T(8,128)}, f32[2,16,2304]{2,1,0:T(8,128)}) custom-call(bf16[12,3,384]{2,1,0:T(4,128)(2,1)} %triple.1, bf16[12,384]{1,0:T(8,128)(2,1)} %bitcast.10, bf16[12,1536]{1,0:T(8,128)(2,1)} %inner_w.1, bf16[12,1536]{1,0:T(8,128)(2,1)} %bitcast.9, bf16[2,12]{1,0:T(2,128)(2,1)} %gains.1, ...), custom_call_target="tpu_custom_call" | custom-call | tf_op jit(solution)/shard_map/layer/pallas_call | solution.py:881
  93.1 2.3 %unpack.1 = (f32[2,6]{1,0:T(2,128)}, f32[2,6]{1,0:T(2,128)}, f32[3,6]{1,0:T(4,128)}, f32[1,24]{1,0:T(1,128)}, f32[1,6]{1,0:T(1,128)}, /*index=5*/f32[12,3,384]{2...) custom-call(f32[2,16,2304]{2,1,0:T(8,128)} %get-tuple-element.26.row, ...), custom_call_target="tpu_custom_call" | custom-call | tf_op jit(solution)/shard_map/unpack/pallas_call | solution.py:921
